TPU v7x, 128 devices: a whole 4x4x4 slice. The times are simulated.
128 devices in a mesh: mem: 8 (over z, core), blk: 16 (over x, y).
Axes of the slice: x: 4, y: 4, z: 4, core: 2. Of those that a mesh axis runs over, the one named last changes fastest.
Arguments:
- members: bfloat16 [128, 64, 128, 256], P(('mem', 'blk')), may hold values from -6 to 6
- obs_cell: int32 [64, 128, 128], P('mem', 'blk'), may hold values from 0 to 255
- obs_value: float32 [64, 128, 128], P('mem', 'blk'), may hold values from -8 to 8
- obs_rinv: float32 [64, 128, 128], P('mem', 'blk'), may hold values from 0.25 to 4
- obs_count: int32 [64, 128], P('mem', 'blk'), may hold values from 1 to 128
- loc_pattern: int32 [64, 128, 9], P('mem', 'blk'), may hold values 0 or 1
Outputs:
- analysis: bfloat16 [128, 64, 128, 256], P(('mem', 'blk'))
All inputs are finite; a program needn't handle non-finite values. No bound on the sum of `loc_pattern` on one device may be relied on, other than what follows from the above.
Results may differ from a plain program's by a relative error of at most 0.013.
Values may be sent and summed in bfloat16 or wider, within the bound.
No kernel may reach another device: no remote copies, remote signals or barrier semaphores. Data moves between devices by JAX's collectives and lax.ppermute only.
A program may use at most 128 MiB of HBM per device.

v0:
```python
import jax
import jax.numpy as jnp
from jax import lax
from jax.sharding import PartitionSpec as P

NS_STEPS = 5


TAPER_WEIGHTS = (0.3, 0.6, 0.3, 0.6, 1.0, 0.6, 0.3, 0.6, 0.3)
INFLATION = 1.1


def with_halo(shard, sides, width):
    for axis, dim in sides:
        count, length = (lax.axis_size(axis), shard.shape[dim])
        up = [(i, (i + 1) % count) for i in range(count)]
        down = [(j, i) for i, j in up]
        last = lax.slice_in_dim(shard, length - width, length, axis=dim)
        leading = lax.slice_in_dim(shard, 0, width, axis=dim)
        before = lax.ppermute(last, axis, up)
        after = lax.ppermute(leading, axis, down)
        shard = jnp.concatenate([before, shard, after], axis=dim)
    return shard


def observed_values(state, obs_cell):
    cell_count = state.shape[3]
    cell_ids = lax.broadcasted_iota(jnp.int32, (1, 1, cell_count, 1), 2)
    selector = (cell_ids == obs_cell[:, :, None, :]).astype(jnp.bfloat16)
    return jnp.einsum("kijc,ijco->ijko", state, selector, preferred_element_type=jnp.float32)


def obs_payload(state, obs_cell, obs_value, obs_rinv, obs_count):
    obs_ens = observed_values(state, obs_cell)
    obs_mean = jnp.mean(obs_ens, axis=2)
    spread_obs = obs_ens - obs_mean[:, :, None]
    departure = obs_value - obs_mean
    live = (lax.broadcasted_iota(jnp.int32, obs_value.shape, 2) < obs_count[:, :, None]).astype(
        jnp.float32
    )
    obs_weight = obs_rinv * live
    return jnp.concatenate([spread_obs, departure[:, :, None], obs_weight[:, :, None]], axis=2)


def analyse_row(three_rows, pattern_row, state_row):
    highest = lax.Precision.HIGHEST
    lon_cols = state_row.shape[0]
    members = state_row.shape[1]
    obs_slots = three_rows.shape[3]
    neighbours = jnp.stack(
        [three_rows[:, offset : offset + lon_cols] for offset in range(3)], axis=1
    )
    neighbours = neighbours.reshape(9, lon_cols, members + 2, obs_slots)
    neighbours = jnp.transpose(neighbours, (1, 2, 0, 3)).reshape(
        lon_cols, members + 2, 9 * obs_slots
    )
    spread_obs = neighbours[:, :members]
    departure = neighbours[:, members]
    taper_row = jnp.asarray(TAPER_WEIGHTS, jnp.float32)[None, :] * pattern_row.astype(jnp.float32)
    obs_weight = neighbours[:, members + 1] * jnp.repeat(taper_row, obs_slots, axis=1)
    scaled = spread_obs * obs_weight[:, None, :]
    identity = jnp.eye(members, dtype=jnp.float32)
    info_matrix = (members - 1) / INFLATION * identity + jnp.einsum(
        "bkp,blp->bkl", scaled, spread_obs, precision=highest
    )
    scale_norm = jnp.sqrt(jnp.sum(info_matrix * info_matrix, axis=(1, 2)))
    iter_p = info_matrix / scale_norm[:, None, None]
    iter_q = jnp.broadcast_to(identity, iter_p.shape)
    for sweep in range(NS_STEPS):
        factor = 1.5 * identity - 0.5 * jnp.einsum(
            "bij,bjk->bik", iter_q, iter_p, precision=highest
        )
        iter_p, iter_q = (
            jnp.einsum("bij,bjk->bik", iter_p, factor, precision=highest),
            jnp.einsum("bij,bjk->bik", factor, iter_q, precision=highest),
        )
    covariance = (
        jnp.einsum("bij,bjk->bik", iter_q, iter_q, precision=highest) / scale_norm[:, None, None]
    )
    gain_in = jnp.einsum("bkp,bp->bk", scaled, departure, precision=highest)
    mean_weights = jnp.einsum("bkl,bl->bk", covariance, gain_in, precision=highest)
    transform = (
        jnp.sqrt((members - 1) / scale_norm)[:, None, None] * iter_q + mean_weights[:, :, None]
    )
    background = state_row.astype(jnp.float32)
    ens_mean = jnp.mean(background, axis=1, keepdims=True)
    perturb = background - ens_mean
    result = ens_mean + jnp.einsum("bik,bic->bkc", transform, perturb, precision=highest)
    return result.astype(jnp.bfloat16)


def shards(members, obs_cell, obs_value, obs_rinv, obs_count, loc_pattern):
    mem_count = lax.axis_size("mem")
    blk_count = lax.axis_size("blk")
    member_dev, lat_all, lon_all, cell_count = members.shape
    lat_rows = lat_all // mem_count
    lon_cols = lon_all // blk_count
    blocks = lax.all_to_all(
        lax.all_to_all(members, "mem", split_axis=1, concat_axis=0, tiled=True),
        "blk",
        split_axis=2,
        concat_axis=0,
        tiled=True,
    )
    lower = (lax.axis_index("mem") > 0).astype(jnp.float32)
    upper = (lax.axis_index("mem") < mem_count - 1).astype(jnp.float32)
    pole_scale = jnp.concatenate([lower[None], jnp.ones((lat_rows,), jnp.float32), upper[None]])
    payload = obs_payload(blocks, obs_cell, obs_value, obs_rinv, obs_count)
    padded = with_halo(payload.astype(jnp.bfloat16), (("mem", 0), ("blk", 1)), 1).astype(
        payload.dtype
    )
    padded = padded * pole_scale[:, None, None, None]
    state_rows = jnp.moveaxis(blocks, 0, 2)

    def one_row(inputs):
        row_index, pattern_row, state_row = inputs
        three_rows = lax.dynamic_slice_in_dim(padded, row_index, 3, 0)
        return analyse_row(three_rows, pattern_row, state_row)

    rows = lax.map(one_row, (jnp.arange(lat_rows, dtype=jnp.int32), loc_pattern, state_rows))
    analysed = jnp.moveaxis(rows, 2, 0)
    grouped = analysed.reshape(blk_count, mem_count, member_dev, lat_rows, lon_cols, cell_count)
    returned = lax.all_to_all(
        lax.all_to_all(grouped, "mem", split_axis=1, concat_axis=3, tiled=True),
        "blk",
        split_axis=0,
        concat_axis=4,
        tiled=True,
    )
    return returned.reshape(member_dev, lat_all, lon_all, cell_count)


def solution(mesh):
    in_specs = (
        P(("mem", "blk"), None, None, None),
        P("mem", "blk", None),
        P("mem", "blk", None),
        P("mem", "blk", None),
        P("mem", "blk"),
        P("mem", "blk", None),
    )
    out_specs = P(("mem", "blk"), None, None, None)
    return jax.shard_map(shards, mesh=mesh, in_specs=in_specs, out_specs=out_specs, check_vma=False)
```

profile of v0, /device:TPU:1, one launch (start us, length us, event | category | flops | bytes accessed | tf_op | source)
XLA Modules:
  0.0 625.5 jit_solution(14958473196074522500)
XLA Ops:
  0.0 56.1 %all_to_all.57 = bf16[1,64,128,256]{3,2,0,1:T(8,128)(2,1)S(1)} all-to-all(bf16[1,64,128,256]{3,2,0,1:T(8,128)(2,1)} %bitcast.189), channel_id=1, replica_groups=mesh['mem'=8,'blk'=16] {'mem'}, dimensions={1} | all-to-all | bytes 8388608 | tf_op jit(solution)/shard_map/all_to_all | solution.py:99
  56.1 4.4 copy.43
  60.5 6.9 %all-to-all-start.1 = ((bf16[8,8,128,256]{3,1,0,2:T(8,128)(2,1)}), bf16[8,8,128,256]{3,1,0,2:T(8,128)(2,1)}, u32[]{:S(2)}, u32[]{:S(2)}) async-start(bf16[8,8,128,256]{3,1,0,2:T(8,128)(2,1)} %copy.43), calls=%async_computation.1 | async-start | bytes 8388608 | tf_op jit(solution)/shard_map/all_to_all | solution.py:98
  67.6 54.6 %all-to-all-done.1 = bf16[8,8,128,256]{3,1,0,2:T(8,128)(2,1)} async-done(((bf16[8,8,128,256]{3,1,0,2:T(8,128)(2,1)}), bf16[8,8,128,256]{3,1,0,2:T(8,128)(2,1)}, u32[]{:S(2)}, u32[]{:S(2)}) %all-to-all-start.1) | async-done | bytes 4194336 | tf_op jit(solution)/shard_map/all_to_all | solution.py:98
  122.3 4.7 bitcast_reduce_fusion
  127.7 3.1 collective-permute-start
  130.8 3.5 collective-permute-done
  134.3 2.8 collective-permute-done.1
  137.2 4.8 collective-permute-start.3
  142.1 5.1 copy.101
  147.2 2.4 collective-permute-done.2
  149.6 4.8 convert_multiply_fusion
  154.4 345.8 %while.11 = (s32[]{:T(128)}, bf16[8,8,128,256]{3,1,0,2:T(8,128)(2,1)}, bf16[8,8,128,256]{3,2,1,0:T(8,128)(2,1)}, s32[8]{0:T(128)S(1)}, f32[10,10,130,128]{3,2,1,...) while((s32[]{:T(128)}, ...), condition=%wide.region_4.5_spmd.clone, body=%wide.region_1.4_spmd.sunk.clone.sunk | while | flops 5259015168 | bytes 122510760 | solution.py:120
  172.9 2.9 constant_dynamic-slice_fusion.4
  177.5 2.6 slice.56
  182.9 7.4 %fusion.192 = f32[8,128,1]{1,2,0:T(1,128)S(1)} fusion(f32[8,128,1152]{2,0,1:T(8,128)} %slice.56, f32[8,1152]{1,0:T(8,128)S(1)} %get-tuple-element.172, f32[8,1152,1]{1,0,2:T(8,128)S(1)} %get-tuple-element.176), kind=kOutput, calls=%fused_computation.30.clone.1 | convolution fusion | flops 15335424 | bytes 4796416 | tf_op jit(solution)/shard_map/while/body/eval_jaxpr/bkp,bp->bk/dot_general | solution.py:80
  190.3 6.2 multiply_reduce_fusion.2
  207.3 1.1 convert_reduce_fusion.2
  208.4 2.3 fusion.194
  214.0 3.0 constant_dynamic-slice_fusion.4
  218.7 2.6 slice.56
  224.1 7.4 %fusion.192 = f32[8,128,1]{1,2,0:T(1,128)S(1)} fusion(f32[8,128,1152]{2,0,1:T(8,128)} %slice.56, f32[8,1152]{1,0:T(8,128)S(1)} %get-tuple-element.172, f32[8,1152,1]{1,0,2:T(8,128)S(1)} %get-tuple-element.176), kind=kOutput, calls=%fused_computation.30.clone.1 | convolution fusion | flops 15335424 | bytes 4796416 | tf_op jit(solution)/shard_map/while/body/eval_jaxpr/bkp,bp->bk/dot_general | solution.py:80
  231.5 6.2 multiply_reduce_fusion.2
  249.6 2.3 fusion.194
  255.3 2.9 constant_dynamic-slice_fusion.4
  259.8 2.6 slice.56
  265.2 7.4 %fusion.192 = f32[8,128,1]{1,2,0:T(1,128)S(1)} fusion(f32[8,128,1152]{2,0,1:T(8,128)} %slice.56, f32[8,1152]{1,0:T(8,128)S(1)} %get-tuple-element.172, f32[8,1152,1]{1,0,2:T(8,128)S(1)} %get-tuple-element.176), kind=kOutput, calls=%fused_computation.30.clone.1 | convolution fusion | flops 15335424 | bytes 4796416 | tf_op jit(solution)/shard_map/while/body/eval_jaxpr/bkp,bp->bk/dot_general | solution.py:80
  272.6 6.2 multiply_reduce_fusion.2
  289.6 1.1 convert_reduce_fusion.2
  290.7 2.3 fusion.194
  296.3 3.0 constant_dynamic-slice_fusion.4
  301.0 2.6 slice.56
  306.4 7.4 %fusion.192 = f32[8,128,1]{1,2,0:T(1,128)S(1)} fusion(f32[8,128,1152]{2,0,1:T(8,128)} %slice.56, f32[8,1152]{1,0:T(8,128)S(1)} %get-tuple-element.172, f32[8,1152,1]{1,0,2:T(8,128)S(1)} %get-tuple-element.176), kind=kOutput, calls=%fused_computation.30.clone.1 | convolution fusion | flops 15335424 | bytes 4796416 | tf_op jit(solution)/shard_map/while/body/eval_jaxpr/bkp,bp->bk/dot_general | solution.py:80
  313.8 6.2 multiply_reduce_fusion.2
  330.7 1.1 convert_reduce_fusion.2
  331.9 2.3 fusion.194
  337.5 3.1 constant_dynamic-slice_fusion.4
  342.3 2.6 slice.56
  347.7 7.4 %fusion.192 = f32[8,128,1]{1,2,0:T(1,128)S(1)} fusion(f32[8,128,1152]{2,0,1:T(8,128)} %slice.56, f32[8,1152]{1,0:T(8,128)S(1)} %get-tuple-element.172, f32[8,1152,1]{1,0,2:T(8,128)S(1)} %get-tuple-element.176), kind=kOutput, calls=%fused_computation.30.clone.1 | convolution fusion | flops 15335424 | bytes 4796416 | tf_op jit(solution)/shard_map/while/body/eval_jaxpr/bkp,bp->bk/dot_general | solution.py:80
  355.1 6.2 multiply_reduce_fusion.2
  372.1 1.1 convert_reduce_fusion.2
  373.2 2.3 fusion.194
  378.8 3.0 constant_dynamic-slice_fusion.4
  383.4 2.6 slice.56
  388.9 7.4 %fusion.192 = f32[8,128,1]{1,2,0:T(1,128)S(1)} fusion(f32[8,128,1152]{2,0,1:T(8,128)} %slice.56, f32[8,1152]{1,0:T(8,128)S(1)} %get-tuple-element.172, f32[8,1152,1]{1,0,2:T(8,128)S(1)} %get-tuple-element.176), kind=kOutput, calls=%fused_computation.30.clone.1 | convolution fusion | flops 15335424 | bytes 4796416 | tf_op jit(solution)/shard_map/while/body/eval_jaxpr/bkp,bp->bk/dot_general | solution.py:80
  396.3 6.2 multiply_reduce_fusion.2
  413.2 1.1 convert_reduce_fusion.2
  414.4 2.3 fusion.194
  420.0 2.9 constant_dynamic-slice_fusion.4
  424.6 2.6 slice.56
  430.0 7.4 %fusion.192 = f32[8,128,1]{1,2,0:T(1,128)S(1)} fusion(f32[8,128,1152]{2,0,1:T(8,128)} %slice.56, f32[8,1152]{1,0:T(8,128)S(1)} %get-tuple-element.172, f32[8,1152,1]{1,0,2:T(8,128)S(1)} %get-tuple-element.176), kind=kOutput, calls=%fused_computation.30.clone.1 | convolution fusion | flops 15335424 | bytes 4796416 | tf_op jit(solution)/shard_map/while/body/eval_jaxpr/bkp,bp->bk/dot_general | solution.py:80
  437.4 6.2 multiply_reduce_fusion.2
  454.3 1.1 convert_reduce_fusion.2
  455.5 2.3 fusion.194
  461.1 3.0 constant_dynamic-slice_fusion.4
  465.8 2.6 slice.56
  471.2 7.4 %fusion.192 = f32[8,128,1]{1,2,0:T(1,128)S(1)} fusion(f32[8,128,1152]{2,0,1:T(8,128)} %slice.56, f32[8,1152]{1,0:T(8,128)S(1)} %get-tuple-element.172, f32[8,1152,1]{1,0,2:T(8,128)S(1)} %get-tuple-element.176), kind=kOutput, calls=%fused_computation.30.clone.1 | convolution fusion | flops 15335424 | bytes 4796416 | tf_op jit(solution)/shard_map/while/body/eval_jaxpr/bkp,bp->bk/dot_general | solution.py:80
  478.6 6.2 multiply_reduce_fusion.2
  496.7 2.3 fusion.194
  500.1 6.7 %copy.50 = bf16[16,8,1,8,8,256]{5,0,4,3,2,1:T(8,128)(2,1)S(1)} copy(bf16[16,8,1,8,8,256]{5,4,3,1,0,2:T(8,128)(2,1)} %bitcast.13) | data formatting | bytes 8388608 | tf_op jit(solution)/shard_map/reshape | solution.py:122
  506.9 57.4 %all_to_all.58 = bf16[16,8,1,8,8,256]{5,0,4,3,2,1:T(8,128)(2,1)S(1)} all-to-all(bf16[16,8,1,8,8,256]{5,0,4,3,2,1:T(8,128)(2,1)S(1)} %copy.50), channel_id=1, replica_groups=mesh['mem'=8,'blk'=16] {'mem'}, dimensions={1} | all-to-all | bytes 8388608 | tf_op jit(solution)/shard_map/all_to_all | solution.py:124
  564.3 1.5 copy.51
  565.8 56.8 %all_to_all.59 = bf16[16,1,1,64,8,256]{5,4,3,2,1,0:T(8,128)(2,1)S(1)} all-to-all(bf16[16,1,1,64,8,256]{5,4,3,2,1,0:T(8,128)(2,1)S(1)} %copy.51), channel_id=1, replica_groups=mesh['mem'=8,'blk'=16] {'blk'}, dimensions={0} | all-to-all | bytes 8388608 | tf_op jit(solution)/shard_map/all_to_all | solution.py:123
  622.5 2.6 copy.100
  (298 shorter events, 137.2 us)
Async XLA Ops:
  60.5 7.0 %copy-start.3 = (f32[8,8,128]{2,1,0:T(8,128)S(1)}, f32[8,8,128]{2,1,0:T(8,128)}, u32[]{:S(2)}) copy-start(f32[8,8,128]{2,1,0:T(8,128)} %param.12) | copy-start | bytes 98308
  60.5 7.0 %copy-start.5 = (s32[8,8]{1,0:T(8,128)S(1)}, s32[8,8]{1,0:T(8,128)}, u32[]{:S(2)}) copy-start(s32[8,8]{1,0:T(8,128)} %param.13) | copy-start | bytes 772
  60.5 61.7 %copy-start.6 = (s32[8,8,128]{2,1,0:T(8,128)S(1)}, s32[8,8,128]{2,1,0:T(8,128)}, u32[]{:S(2)}) copy-start(s32[8,8,128]{2,1,0:T(8,128)} %param.10) | copy-start | bytes 98308
  60.5 61.7 %all-to-all-start.1 = ((bf16[8,8,128,256]{3,1,0,2:T(8,128)(2,1)}), bf16[8,8,128,256]{3,1,0,2:T(8,128)(2,1)}, u32[]{:S(2)}, u32[]{:S(2)}) async-start(bf16[8,8,128,256]{3,1,0,2:T(8,128)(2,1)} %copy.43), calls=%async_computation.1 | async-start | bytes 8388608 | tf_op jit(solution)/shard_map/all_to_all | solution.py:98
  122.3 4.7 copy-start.2
  127.7 6.6 %collective-permute-start = (bf16[1,8,130,128]{3,2,1,0:T(8,128)(2,1)S(1)}, bf16[1,8,130,128]{3,2,1,0:T(8,128)(2,1)S(1)}, u32[]{:S(2)}, u32[]{:S(2)}) collective-permute-start(bf16[1,8,130,128]{3,2,1,0:T(8,128)(2,1)S(1)} %get-tuple-element.113), channel_id=1, source_target_pairs={{0,16},{16,32},{32,48},{48,64},{64,80},{80,96},{96,112},{112,0},{1... | collective-permute-start | bytes 798728 | tf_op jit(solution)/shard_map/ppermute | solution.py:20
  130.8 6.3 %collective-permute-start.1 = (bf16[1,8,130,128]{3,2,1,0:T(8,128)(2,1)S(1)}, bf16[1,8,130,128]{3,2,1,0:T(8,128)(2,1)S(1)}, u32[]{:S(2)}, u32[]{:S(2)}) collective-permute-start(bf16[1,8,130,128]{3,2,1,0:T(8,128)(2,1)S(1)} %get-tuple-element.114), channel_id=1, source_target_pairs={{16,0},{32,16},{48,32},{64,48},{80,64},{96,80},{112,96},{0,112},{1... | collective-permute-start | bytes 798728 | tf_op jit(solution)/shard_map/ppermute | solution.py:21
  137.1 12.4 %collective-permute-start.2 = (bf16[10,1,130,128]{3,2,1,0:T(8,128)(2,1)S(1)}, bf16[10,1,130,128]{3,2,1,0:T(8,128)(2,1)}, u32[]{:S(2)}, u32[]{:S(2)}) collective-permute-start(bf16[10,1,130,128]{3,2,1,0:T(8,128)(2,1)S(1)} %get-tuple-element.111), channel_id=1, source_target_pairs={{0,1},{1,2},{2,3},{3,4},{4,5},{5,6},{6,7},{7,8},{8,9},{9,10},{10,1... | collective-permute-start | bytes 998408 | tf_op jit(solution)/shard_map/ppermute | solution.py:20
  137.2 12.3 %collective-permute-start.3 = (bf16[10,1,130,128]{3,2,1,0:T(8,128)(2,1)S(1)}, bf16[10,1,130,128]{3,2,1,0:T(8,128)(2,1)}, u32[]{:S(2)}, u32[]{:S(2)}) collective-permute-start(bf16[10,1,130,128]{3,2,1,0:T(8,128)(2,1)S(1)} %get-tuple-element.112), channel_id=1, source_target_pairs={{1,0},{2,1},{3,2},{4,3},{5,4},{6,5},{7,6},{8,7},{9,8},{10,9},{11,1... | collective-permute-start | bytes 998408 | tf_op jit(solution)/shard_map/ppermute | solution.py:21
  147.2 7.2 %copy-start.4 = (f32[9]{0:T(128)S(1)}, f32[9]{0:T(128)}, u32[]{:S(2)}) copy-start(f32[9]{0:T(128)} %constant.51.clone..sunk.2) | copy-start | bytes 112
  177.5 3.7 copy-start.1
  181.9 8.4 %copy-start = (f32[8,128,1152]{2,0,1:T(8,128)S(1)}, f32[8,128,1152]{2,0,1:T(8,128)}, u32[]{:S(2)}) copy-start(f32[8,128,1152]{2,0,1:T(8,128)} %slice.56) | copy-start | bytes 14155780 | tf_op jit(solution)/shard_map/while
  218.7 3.7 copy-start.1
  223.1 8.4 %copy-start = (f32[8,128,1152]{2,0,1:T(8,128)S(1)}, f32[8,128,1152]{2,0,1:T(8,128)}, u32[]{:S(2)}) copy-start(f32[8,128,1152]{2,0,1:T(8,128)} %slice.56) | copy-start | bytes 14155780 | tf_op jit(solution)/shard_map/while
  259.8 3.7 copy-start.1
  264.2 8.4 %copy-start = (f32[8,128,1152]{2,0,1:T(8,128)S(1)}, f32[8,128,1152]{2,0,1:T(8,128)}, u32[]{:S(2)}) copy-start(f32[8,128,1152]{2,0,1:T(8,128)} %slice.56) | copy-start | bytes 14155780 | tf_op jit(solution)/shard_map/while
  300.9 3.7 copy-start.1
  305.4 8.4 %copy-start = (f32[8,128,1152]{2,0,1:T(8,128)S(1)}, f32[8,128,1152]{2,0,1:T(8,128)}, u32[]{:S(2)}) copy-start(f32[8,128,1152]{2,0,1:T(8,128)} %slice.56) | copy-start | bytes 14155780 | tf_op jit(solution)/shard_map/while
  342.3 3.7 copy-start.1
  346.7 8.4 %copy-start = (f32[8,128,1152]{2,0,1:T(8,128)S(1)}, f32[8,128,1152]{2,0,1:T(8,128)}, u32[]{:S(2)}) copy-start(f32[8,128,1152]{2,0,1:T(8,128)} %slice.56) | copy-start | bytes 14155780 | tf_op jit(solution)/shard_map/while
  383.4 3.7 copy-start.1
  387.9 8.4 %copy-start = (f32[8,128,1152]{2,0,1:T(8,128)S(1)}, f32[8,128,1152]{2,0,1:T(8,128)}, u32[]{:S(2)}) copy-start(f32[8,128,1152]{2,0,1:T(8,128)} %slice.56) | copy-start | bytes 14155780 | tf_op jit(solution)/shard_map/while
  424.5 3.7 copy-start.1
  429.0 8.4 %copy-start = (f32[8,128,1152]{2,0,1:T(8,128)S(1)}, f32[8,128,1152]{2,0,1:T(8,128)}, u32[]{:S(2)}) copy-start(f32[8,128,1152]{2,0,1:T(8,128)} %slice.56) | copy-start | bytes 14155780 | tf_op jit(solution)/shard_map/while
  465.8 3.7 copy-start.1
  470.2 8.4 %copy-start = (f32[8,128,1152]{2,0,1:T(8,128)S(1)}, f32[8,128,1152]{2,0,1:T(8,128)}, u32[]{:S(2)}) copy-start(f32[8,128,1152]{2,0,1:T(8,128)} %slice.56) | copy-start | bytes 14155780 | tf_op jit(solution)/shard_map/while
where the time goes:
time: 636 us; the launch traced here: 625 us
  matrix products  216 us (34%)
  blocking collectives  170 us (27%)
  local copies, waits for them, and re-layouts  96.5 us (15%)
  waiting for transfers between devices  63.3 us (10%)
  other arithmetic  32.6 us (5%)
  loops' own time  31.3 us (5%)
  starting transfers between devices  14.9 us (2%)
    dot_general x8, matrix products, analyse_row(): gain_in = jnp.einsum('bkp,bp->bk', scaled, departure, precision=highest)  58.9 us
    all_to_all x1, blocking collectives, shards(): lax.all_to_all(grouped, 'mem', split_axis=1, concat_axis=3, tiled=True)  57.4 us
    all_to_all x1, blocking collectives, shards(): lax.all_to_all(lax.all_to_all(grouped, 'mem', split_axis=1, concat_axis=3...  56.8 us
    all_to_all x1, blocking collectives, shards(): lax.all_to_all(members, 'mem', split_axis=1, concat_axis=0, tiled=True)  56.1 us
    all_to_all x1, waiting for transfers between devices, shards(): lax.all_to_all(lax.all_to_all(members, 'mem', split_axis=1, concat_axis=0...  54.6 us
    dot_general x8, matrix products, analyse_row(): jnp.einsum('bkp,blp->bkl', scaled, spread_obs, precision=highest)  49.3 us
    another operation x1, loops' own time, shards(): lax.map(one_row, (jnp.arange(lat_rows, dtype=jnp.int32), loc_pattern, sta...  31.3 us
    dot_general x40, matrix products, analyse_row(): jnp.einsum('bij,bjk->bik', iter_q, iter_p, precision=highest)  25.9 us
  transfers between devices with their start and end apart: 5, of which 4 were waited for; matrix products, arithmetic and copies ran while one was open for 1% of the time, Pallas kernels for 0%

commit v1 on v0

v1 whole, which is shorter than its diff:
```python
import jax
import jax.numpy as jnp
from jax import lax
from jax.experimental import pallas as pl
from jax.experimental.pallas import tpu as pltpu
from jax.sharding import PartitionSpec as P

NS_STEPS = 5
TAPER_WEIGHTS = (0.3, 0.6, 0.3, 0.6, 1.0, 0.6, 0.3, 0.6, 0.3)
INFLATION = 1.1
F32 = jnp.float32
BF16 = jnp.bfloat16
PAD = 16
LANES = 128
AXES = ("mem", "blk")
VMEM_LIMIT = 48 * 1024 * 1024


def select_kernel(x_ref, cell_ref, value_ref, root_ref, xt_ref, gh_ref, wide):
    members, group, cells = x_ref.shape
    slots = cell_ref.shape[1]
    for k in range(0, members, 16):
        part = x_ref[k : k + 16].astype(F32).reshape(16 * group, cells)
        for h in range(cells // LANES):
            wide[h, k * group : (k + 16) * group, :] = part[:, h * LANES : (h + 1) * LANES]
    ids = lax.broadcasted_iota(jnp.int32, (cells, slots), 0)
    pad_row = lax.broadcasted_iota(jnp.int32, (PAD, slots), 0)

    def block(b, carry):
        state = jnp.concatenate(
            [
                wide[h, pl.ds(b, members, stride=group), :].astype(BF16)
                for h in range(cells // LANES)
            ],
            axis=1,
        )
        xt_ref[b] = state
        selector = (ids == cell_ref[pl.ds(b, 1), :]).astype(BF16)
        obs = jnp.dot(state, selector, preferred_element_type=F32)
        mean = jnp.sum(obs, axis=0, keepdims=True) * (1.0 / members)
        root = root_ref[pl.ds(b, 1), :]
        rooted = ((obs - mean) * root).astype(BF16)
        depart = (value_ref[pl.ds(b, 1), :] - mean) * root
        high = depart.astype(BF16).astype(F32)
        extra = jnp.where(pad_row == 0, high, jnp.where(pad_row == 1, depart - high, 0.0))
        left = jnp.concatenate([rooted, extra.astype(BF16)], axis=0)
        gram = lax.dot_general(
            left, rooted, (((1,), (1,)), ((), ())), preferred_element_type=F32
        )
        gain = gram[members : members + 1] + gram[members + 1 : members + 2]
        gain_high = gain.astype(BF16).astype(F32)
        tail = jnp.where(pad_row == 0, gain_high, jnp.where(pad_row == 1, gain - gain_high, 0.0))
        gh_ref[b, :members] = gram[:members].astype(BF16)
        gh_ref[b, members:] = tail.astype(BF16)
        return carry

    lax.fori_loop(0, group, block, 0, unroll=2)


def select(state, cell, value, root):
    members, blocks, cells = state.shape
    slots = cell.shape[1]
    group = 16
    row = pl.BlockSpec((group, slots), lambda i: (i, 0))
    return pl.pallas_call(
        select_kernel,
        grid=(blocks // group,),
        in_specs=[pl.BlockSpec((members, group, cells), lambda i: (0, i, 0)), row, row, row],
        out_specs=[
            pl.BlockSpec((group, members, cells), lambda i: (i, 0, 0)),
            pl.BlockSpec((group, members + PAD, members), lambda i: (i, 0, 0)),
        ],
        out_shape=[
            jax.ShapeDtypeStruct((blocks, members, cells), BF16),
            jax.ShapeDtypeStruct((blocks, members + PAD, members), BF16),
        ],
        scratch_shapes=[pltpu.VMEM((cells // LANES, members * group, LANES), F32)],
        compiler_params=pltpu.CompilerParams(vmem_limit_bytes=VMEM_LIMIT),
        cost_estimate=pl.CostEstimate(
            flops=blocks * 2 * members * slots * (cells + members),
            bytes_accessed=blocks * (4 * members * cells + 2 * (members + PAD) * members),
            transcendentals=0,
        ),
        name="select",
    )(state, cell, value, root)


def analyse_lat(gh, xt, weight, first, pq_f, pq_b, bd, wide, stride, offset):
    cols, members, cells = xt.shape
    c = members
    pairs = cols // 2
    eye = (
        lax.broadcasted_iota(jnp.int32, (members, members), 0)
        == lax.broadcasted_iota(jnp.int32, (members, members), 1)
    )
    ident = eye.astype(F32)
    norms = []
    gains = []
    for j in range(cols):
        acc = None
        for n in range(9):
            term = gh[n // 3, j + n % 3].astype(F32) * weight[(first + j) * 9 + n]
            acc = term if acc is None else acc + term
        info = acc[:members] + (members - 1) / INFLATION * ident
        gains.append(acc[members : members + 1] + acc[members + 1 : members + 2])
        inv = lax.rsqrt(jnp.sum(jnp.sum(info * info, axis=0, keepdims=True), axis=1, keepdims=True))
        norms.append(inv)
        p = info * inv
        third = p * (1.0 / 3.0)
        lanes = slice((j % 2) * c, (j % 2) * c + c)
        pq_f[j // 2, :c, lanes] = p
        pq_b[j // 2, :c, lanes] = p.astype(BF16)
        q = ident - third
        pq_f[j // 2, c:, lanes] = q
        pq_b[j // 2, c:, lanes] = q.astype(BF16)
        bd[j // 2, lanes, lanes] = third.astype(BF16)
    for t in range(pairs):
        p = pq_f[t, :c] - jnp.dot(pq_b[t, :c], bd[t], preferred_element_type=F32)
        pq_f[t, :c] = p
        pq_b[t, :c] = p.astype(BF16)
    for step in range(1, NS_STEPS):
        for t in range(pairs):
            bd[t, :c, :c] = pq_b[t, :c, :c]
            bd[t, c:, c:] = pq_b[t, :c, c:]
        scale = 1.5 ** (2 * step) / 3.0
        for t in range(pairs):
            prod = jnp.dot(pq_b[t, c:], bd[t], preferred_element_type=F32) * scale
            bd[t, :c, :c] = prod[:, :c].astype(BF16)
            bd[t, c:, c:] = prod[:, c:].astype(BF16)
        start = 0 if step < NS_STEPS - 1 else c
        for t in range(pairs):
            new = pq_f[t, start:] - jnp.dot(pq_b[t, start:], bd[t], preferred_element_type=F32)
            pq_f[t, start:] = new
            if start == 0:
                pq_b[t] = new.astype(BF16)
    ones = jnp.full((PAD, members), 1.0 / members, BF16)
    growth = 1.5**NS_STEPS
    for j in range(cols):
        lanes = slice((j % 2) * c, (j % 2) * c + c)
        q = pq_f[j // 2, c:, lanes] * growth
        inv = norms[j]
        column = jnp.sum(q * gains[j], axis=1, keepdims=True)
        weights_row = jnp.sum(q * column, axis=0, keepdims=True) * inv
        transform = (q * jnp.sqrt((members - 1.0) * inv) + weights_row).astype(BF16)
        rest = 1.0 - jnp.sum(transform.astype(F32), axis=1, keepdims=True)
        left = jnp.concatenate([transform, ones], axis=0)
        out = jnp.dot(left, xt[j], preferred_element_type=F32)
        out = out[:members] + rest * out[members : members + 1]
        for h in range(cells // LANES):
            wide[h, pl.ds(offset + j, members, stride=stride), :] = (
                out[:, h * LANES : (h + 1) * LANES]
            )


def analyse(rows, weight, sources, plan, members, cols, cells):
    count = len(rows)
    blocks = count * cols
    c = members

    def kernel(*refs):
        weight_ref = refs[0]
        src = refs[1 : 1 + len(sources)]
        out_ref, gh, xt, pq_f, pq_b, bd, wide, sem = refs[1 + len(sources) :]
        handles = []
        for i in range(count):
            mine = []
            for which, index, kind, place in plan[i]:
                if kind == "x":
                    dst = xt.at[i]
                elif kind == "own":
                    dst = gh.at[i, place, pl.ds(1, cols)]
                else:
                    dst = gh.at[i, place, pl.ds(kind[0], kind[1])]
                handle = pltpu.make_async_copy(src[which].at[index], dst, sem.at[i])
                handle.start()
                mine.append(handle)
            handles.append(mine)
        bd[...] = jnp.zeros_like(bd)
        for i in range(count):
            for handle in handles[i]:
                handle.wait()

        def lat(i, carry):
            first = jnp.where(i == 0, rows[0], rows[1]) * cols if count == 2 else rows[0] * cols
            analyse_lat(
                gh.at[i], xt.at[i], weight_ref, first, pq_f, pq_b, bd, wide,
                blocks, i * cols,
            )
            return carry

        lax.fori_loop(0, count, lat, 0)
        for k in range(0, members, 16):
            for h in range(cells // LANES):
                part = wide[h, k * blocks : (k + 16) * blocks, :].reshape(16, blocks, LANES)
                out_ref[k : k + 16, :, h * LANES : (h + 1) * LANES] = part.astype(BF16)

    any_spec = pl.BlockSpec(memory_space=pl.ANY)
    return pl.pallas_call(
        kernel,
        in_specs=[pl.BlockSpec(memory_space=pltpu.SMEM)] + [any_spec] * len(sources),
        out_specs=pl.BlockSpec(memory_space=pltpu.VMEM),
        out_shape=jax.ShapeDtypeStruct((members, blocks, cells), BF16),
        scratch_shapes=[
            pltpu.VMEM((count, 3, cols + 2, members + PAD, members), BF16),
            pltpu.VMEM((count, cols, members, cells), BF16),
            pltpu.VMEM((cols // 2, 2 * c, 2 * c), F32),
            pltpu.VMEM((cols // 2, 2 * c, 2 * c), BF16),
            pltpu.VMEM((cols // 2, 2 * c, 2 * c), BF16),
            pltpu.VMEM((cells // LANES, members * blocks, LANES), F32),
            pltpu.SemaphoreType.DMA((count,)),
        ],
        compiler_params=pltpu.CompilerParams(vmem_limit_bytes=VMEM_LIMIT),
        cost_estimate=pl.CostEstimate(
            flops=blocks * 2 * 14 * members**3,
            bytes_accessed=blocks * 4 * members * cells,
            transcendentals=0,
        ),
        name="analyse",
    )(weight, *sources)


def shift(value, axis, step, wrap):
    count = lax.axis_size(axis)
    pairs = [(i, (i + step) % count) for i in range(count) if wrap or 0 <= i + step < count]
    return lax.ppermute(value, axis, pairs)


def shards(members, obs_cell, obs_value, obs_rinv, obs_count, loc_pattern):
    mem_count = lax.axis_size("mem")
    blk_count = lax.axis_size("blk")
    devices = mem_count * blk_count
    lat_all, lon_all, cells = members.shape[1:]
    lat, lon = lat_all // mem_count, lon_all // blk_count
    slots = obs_cell.shape[2]

    live = lax.broadcasted_iota(jnp.int32, obs_rinv.shape, 2) < obs_count[:, :, None]
    root = jnp.sqrt(jnp.where(live, obs_rinv, 0.0))
    weight = (
        jnp.asarray(TAPER_WEIGHTS, F32) * loc_pattern.astype(F32)
    ).reshape(lat * lon * 9)

    grouped = members.reshape(mem_count, lat, blk_count, lon, cells).transpose(0, 2, 1, 3, 4)
    grouped = grouped.reshape(devices, lat * lon, cells)
    arrived = lax.all_to_all(grouped, AXES, split_axis=0, concat_axis=0, tiled=True)
    xt, gh = select(
        arrived,
        obs_cell.reshape(lat * lon, slots),
        obs_value.reshape(lat * lon, slots),
        root.reshape(lat * lon, slots),
    )
    rank = gh.shape[1:]
    xt = xt.reshape(lat, lon, devices, cells)
    gh = gh.reshape(lat, lon, *rank)
    west = shift(gh[:, lon - 1], "blk", 1, True)
    east = shift(gh[:, 0], "blk", -1, True)

    def full_row(r):
        return jnp.concatenate([west[r][None], gh[r], east[r][None]], axis=0)

    south = shift(full_row(lat - 1), "mem", 1, False)
    north = shift(full_row(0), "mem", -1, False)
    sources = [xt, gh, west, east, south, north]
    parts = []
    for r in range(0, lat, 2):
        rows = (r, r + 1)
        plan = []
        for row in rows:
            steps = [(0, row, "x", None)]
            for a in range(3):
                at = row + a - 1
                if at < 0:
                    steps.append((4, slice(None), (0, lon + 2), a))
                elif at >= lat:
                    steps.append((5, slice(None), (0, lon + 2), a))
                else:
                    steps.append((1, at, "own", a))
                    steps.append((2, pl.ds(at, 1), (0, 1), a))
                    steps.append((3, pl.ds(at, 1), (lon + 1, 1), a))
            plan.append(steps)
        parts.append(analyse(rows, weight, sources, plan, devices, lon, cells))
    result = jnp.concatenate(parts, axis=1)
    returned = lax.all_to_all(result, AXES, split_axis=0, concat_axis=0, tiled=True)
    returned = returned.reshape(mem_count, blk_count, lat, lon, cells).transpose(0, 2, 1, 3, 4)
    return returned.reshape(1, lat_all, lon_all, cells)


def solution(mesh):
    in_specs = (
        P(AXES, None, None, None),
        P("mem", "blk", None),
        P("mem", "blk", None),
        P("mem", "blk", None),
        P("mem", "blk"),
        P("mem", "blk", None),
    )
    out_specs = P(AXES, None, None, None)
    return jax.shard_map(shards, mesh=mesh, in_specs=in_specs, out_specs=out_specs, check_vma=False)
```

time: 636 us -> 211 us (0.33); the launches traced: 625 us -> 211 us
  matrix products: 216 us -> 0 us
  blocking collectives: 170 us -> 55.4 us
  local copies, waits for them, and re-layouts: 96.5 us -> 9.29 us
  Pallas kernels: 0 us -> 54.2 us
  loops' own time: 31.3 us -> 0 us
  other arithmetic: 32.6 us -> 2.32 us
    dot_general x153 -> x0, matrix products: 216 us -> none  [the longest x8 58.9 us: analyse_row(): gain_in = jnp.einsum('bkp,bp->bk', scaled, departure, precision=highest)]
    all_to_all x3 -> x1, blocking collectives: 170 us -> 55.4 us  [shards(): lax.all_to_all(result, AXES, split_axis=0, concat_axis=0, tiled=True)]
    pallas_call x0 -> x5, Pallas kernels: none -> 54.2 us  [the longest x4 37.1 us: analyse(): pl.pallas_call(kernel, in_specs=[pl.BlockSpec(memory_space=pltpu.SMEM)] +...]
    slice x16 -> x3, local copies, waits for them, and re-layouts: 44.7 us -> 0.05 us  [full_row(): return jnp.concatenate([west[r][None], gh[r], east[r][None]], axis=0)]
    another operation x1 -> x0, loops' own time: 31.3 us -> none  [shards(): lax.map(one_row, (jnp.arange(lat_rows, dtype=jnp.int32), loc_pattern, sta...]
    all_to_all x4 -> x0, local copies, waits for them, and re-layouts: 13.6 us -> none  [the longest x1 5.12 us: shards(): lax.all_to_all(lax.all_to_all(members, 'mem', split_axis=1, concat_axis=0...]
    mul x25 -> x1, other arithmetic: 10.6 us -> 0.01 us  [shards(): jnp.asarray(TAPER_WEIGHTS, F32) * loc_pattern.astype(F32)]
    while x40 -> x0, local copies, waits for them, and re-layouts: 10.6 us -> none
  transfers between devices with their start and end apart: 5 -> 5, of which waited for: 4 -> 5; matrix products, arithmetic and copies ran while one was open for 1% -> 1% of each run, Pallas kernels for 0% -> 0%
where the time goes in v1:
time: 211 us
  waiting for transfers between devices  69.3 us (33%)
  blocking collectives  55.4 us (26%)
  Pallas kernels  54.2 us (26%)
  starting transfers between devices  20.2 us (10%)
  local copies, waits for them, and re-layouts  9.29 us (4%)
  other arithmetic  2.32 us (1%)
    all_to_all x1, blocking collectives, shards(): lax.all_to_all(result, AXES, split_axis=0, concat_axis=0, tiled=True)  55.4 us
    all_to_all x1, waiting for transfers between devices, shards(): lax.all_to_all(grouped, AXES, split_axis=0, concat_axis=0, tiled=True)  52.2 us
    pallas_call x4, Pallas kernels, analyse(): pl.pallas_call(kernel, in_specs=[pl.BlockSpec(memory_space=pltpu.SMEM)] +...  37.1 us
    ppermute x4, waiting for transfers between devices, shift(): return lax.ppermute(value, axis, pairs)  17.1 us
    pallas_call x1, Pallas kernels, select(): pl.pallas_call(select_kernel, grid=(blocks // group,), in_specs=[pl.Block...  17 us
    all_to_all x1, starting transfers between devices, shards(): lax.all_to_all(grouped, AXES, split_axis=0, concat_axis=0, tiled=True)  12 us
    ppermute x4, starting transfers between devices, shift(): return lax.ppermute(value, axis, pairs)  8.22 us
    reshape x1, local copies, waits for them, and re-layouts, shards(): members.reshape(mem_count, lat, blk_count, lon, cells)  4.79 us
  transfers between devices with their start and end apart: 5, of which 5 were waited for; matrix products, arithmetic and copies ran while one was open for 1% of the time, Pallas kernels for 0%

profile of v1, /device:TPU:1, one launch (start us, length us, event | category | flops | bytes accessed | tf_op | source)
XLA Modules:
  0.0 210.8 jit_solution(11760060741537623322)
XLA Ops:
  0.0 4.8 %copy.14 = bf16[8,8,16,8,256]{4,3,1,2,0:T(8,128)(2,1)} copy(bf16[8,8,16,8,256]{4,3,2,1,0:T(8,128)(2,1)} %bitcast.35) | data formatting | bytes 8388608 | tf_op jit(solution)/shard_map/reshape | solution.py:242
  4.8 0.0 copy-start.4
  4.8 0.0 copy-start.6
  4.8 0.0 copy-start.2
  4.8 0.0 copy-start.3
  4.8 12.0 %all-to-all-start = ((bf16[128,64,256]{2,1,0:T(8,128)(2,1)}), bf16[128,64,256]{2,1,0:T(8,128)(2,1)}, u32[]{:S(2)}, u32[]{:S(2)}) async-start(bf16[128,64,256]{2,1,0:T(8,128)(2,1)} %bitcast.33), calls=%async_computation | async-start | bytes 8388608 | tf_op jit(solution)/shard_map/all_to_all | solution.py:244
  16.8 0.0 copy-done.4
  16.8 0.0 copy-done.6
  16.8 0.1 sqrt_bitcast_fusion.root_ref
  16.9 52.2 %all-to-all-done.x_ref = bf16[128,64,256]{2,1,0:T(8,128)(2,1)} async-done(((bf16[128,64,256]{2,1,0:T(8,128)(2,1)}), bf16[128,64,256]{2,1,0:T(8,128)(2,1)}, u32[]{:S(2)}, u32[]{:S(2)}) %all-to-all-start) | async-done | bytes 4194336 | tf_op jit(solution)/shard_map/all_to_all | solution.py:244
  69.1 0.0 copy-done.2
  69.1 0.0 copy-done.3
  69.1 0.0 copy-start.5
  69.1 0.0 copy-start.7
  69.1 17.0 %select.1 = (bf16[64,128,256]{2,1,0:T(8,128)(2,1)}, bf16[64,144,128]{2,1,0:T(8,128)(2,1)S(1)}) custom-call(bf16[128,64,256]{2,1,0:T(8,128)(2,1)} %all-to-all-done.x_ref, s32[64,128]{1,0:T(8,128)S(1)} %bitcast.27, f32[64,128]{1,0:T(8,128)S(1)} %bitcast.28, f32[64,128]{1,0:T(8,128)S(1)} %sqrt_bitcast_fusion.root_ref), custom_call_target="tpu_custom_call" | custom-call | flops 805306368 | bytes 10747904 | tf_op jit(solution)/shard_map/select/pallas_call | solution.py:65
  86.2 2.0 collective-permute-start.1
  88.1 0.0 collective-permute-start
  88.2 6.7 %collective-permute-done.1.refs_4_ = bf16[8,144,128]{2,1,0:T(8,128)(2,1)S(1)} collective-permute-done((bf16[8,144,128]{2,1,0:T(8,128)(2,1)S(1)}, bf16[8,144,128]{2,1,0:T(8,128)(2,1)S(1)}, u32[]{:S(2)}, u32[]{:S(2)}) %collective-permute-start.1) | collective-permute-done | bytes 294944 | tf_op jit(solution)/shard_map/ppermute | solution.py:225
  94.9 3.6 %collective-permute-done.refs_3_ = bf16[8,144,128]{2,1,0:T(8,128)(2,1)S(1)} collective-permute-done((bf16[8,144,128]{2,1,0:T(8,128)(2,1)S(1)}, bf16[8,144,128]{2,1,0:T(8,128)(2,1)S(1)}, u32[]{:S(2)}, u32[]{:S(2)}) %collective-permute-start) | collective-permute-done | bytes 294944 | tf_op jit(solution)/shard_map/ppermute | solution.py:225
  98.5 0.0 copy-start
  98.5 0.7 copy-done
  99.3 0.8 pad_maximum_fusion.1
  100.1 4.2 %collective-permute-start.2 = (bf16[10,144,128]{2,1,0:T(8,128)(2,1)}, bf16[10,144,128]{2,1,0:T(8,128)(2,1)S(1)}, u32[]{:S(2)}, u32[]{:S(2)}) collective-permute-start(bf16[10,144,128]{2,1,0:T(8,128)(2,1)} %pad_maximum_fusion.1), channel_id=1, source_target_pairs={{0,16},{16,32},{32,48},{48,64},{64,80},{80,96},{96,112},{1,17},{17... | collective-permute-start | bytes 1105928 | tf_op jit(solution)/shard_map/ppermute | solution.py:225
  104.2 0.8 pad_maximum_fusion.2
  105.0 2.1 collective-permute-start.3
  107.1 0.0 copy-done.5
  107.1 0.0 copy-done.7
  107.2 0.1 reshape.36.refs_0_
  107.3 1.7 collective-permute-done.2.refs_5_
  109.0 5.1 %collective-permute-done.3.refs_6_ = bf16[10,144,128]{2,1,0:T(8,128)(2,1)S(1)} collective-permute-done((bf16[10,144,128]{2,1,0:T(8,128)(2,1)}, bf16[10,144,128]{2,1,0:T(8,128)(2,1)S(1)}, u32[]{:S(2)}, u32[]{:S(2)}) %collective-permute-start.3) | collective-permute-done | bytes 368672 | tf_op jit(solution)/shard_map/ppermute | solution.py:225
  114.1 0.0 copy-start.1
  114.1 1.0 copy-done.1
  115.0 9.3 %analyse.7 = bf16[128,16,256]{2,1,0:T(8,128)(2,1)S(1)} custom-call(f32[576]{0:T(1024)S(1)} %reshape.36.refs_0_, bf16[8,8,128,256]{3,2,1,0:T(8,128)(2,1)} %bitcast.29, bf16[8,8,144,128]{3,2,1,0:T(8,128)(2,1)S(1)} %bitcast.23, bf16[8,144,128]{2,1,0:T(8,128)(2,1)S(1)} %copy-done.1, bf16[8,144,128]{2,1,0:T(8,128)(2,1)S(1)} %collective-permute-done.1.refs_4_, ...), custom_call_target="tpu_custom_call" | custom-call | flops 939524096 | bytes 2097152 | tf_op jit(solution)/shard_map/analyse/pallas_call | solution.py:198
  124.3 9.3 %analyse.6 = bf16[128,16,256]{2,1,0:T(8,128)(2,1)S(1)} custom-call(f32[576]{0:T(1024)S(1)} %reshape.36.refs_0_, bf16[8,8,128,256]{3,2,1,0:T(8,128)(2,1)} %bitcast.30, bf16[8,8,144,128]{3,2,1,0:T(8,128)(2,1)S(1)} %bitcast.24, bf16[8,144,128]{2,1,0:T(8,128)(2,1)S(1)} %copy-done.1, bf16[8,144,128]{2,1,0:T(8,128)(2,1)S(1)} %collective-permute-done.1.refs_4_, ...), custom_call_target="tpu_custom_call" | custom-call | flops 939524096 | bytes 2097152 | tf_op jit(solution)/shard_map/analyse/pallas_call | solution.py:198
  133.6 9.3 %analyse.5 = bf16[128,16,256]{2,1,0:T(8,128)(2,1)S(1)} custom-call(f32[576]{0:T(1024)S(1)} %reshape.36.refs_0_, bf16[8,8,128,256]{3,2,1,0:T(8,128)(2,1)} %bitcast.31, bf16[8,8,144,128]{3,2,1,0:T(8,128)(2,1)S(1)} %bitcast.25, bf16[8,144,128]{2,1,0:T(8,128)(2,1)S(1)} %copy-done.1, bf16[8,144,128]{2,1,0:T(8,128)(2,1)S(1)} %collective-permute-done.1.refs_4_, ...), custom_call_target="tpu_custom_call" | custom-call | flops 939524096 | bytes 2097152 | tf_op jit(solution)/shard_map/analyse/pallas_call | solution.py:198
  142.9 9.3 %analyse.4 = bf16[128,16,256]{2,1,0:T(8,128)(2,1)S(1)} custom-call(f32[576]{0:T(1024)S(1)} %reshape.36.refs_0_, bf16[8,8,128,256]{3,2,1,0:T(8,128)(2,1)} %bitcast.32, bf16[8,8,144,128]{3,2,1,0:T(8,128)(2,1)S(1)} %bitcast.26, bf16[8,144,128]{2,1,0:T(8,128)(2,1)S(1)} %copy-done.1, bf16[8,144,128]{2,1,0:T(8,128)(2,1)S(1)} %collective-permute-done.1.refs_4_, ...), custom_call_target="tpu_custom_call" | custom-call | flops 939524096 | bytes 2097152 | tf_op jit(solution)/shard_map/analyse/pallas_call | solution.py:198
  152.2 0.6 pad_maximum_fusion
  152.8 55.4 %all_to_all.10 = bf16[128,64,256]{2,1,0:T(8,128)(2,1)S(1)} all-to-all(bf16[128,64,256]{2,1,0:T(8,128)(2,1)S(1)} %pad_maximum_fusion), channel_id=1, replica_groups=mesh['mem'=8,'blk'=16] {'mem','blk'}, dimensions={0} | all-to-all | bytes 8388608 | tf_op jit(solution)/shard_map/all_to_all | solution.py:282
  208.2 2.6 %copy.17 = bf16[8,8,16,8,256]{4,3,2,1,0:T(8,128)(2,1)} copy(bf16[8,8,16,8,256]{4,3,1,2,0:T(8,128)(2,1)S(1)} %bitcast.34) | data formatting | bytes 8388608 | tf_op jit(solution)/shard_map/transpose | solution.py:283
  (5 shorter events, 0.1 us)
Async XLA Ops:
  4.8 12.0 %copy-start.4 = (f32[8,8,128]{2,1,0:T(8,128)S(1)}, f32[8,8,128]{2,1,0:T(8,128)}, u32[]{:S(2)}) copy-start(f32[8,8,128]{2,1,0:T(8,128)} %param.10) | copy-start | bytes 98308
  4.8 12.0 %copy-start.6 = (s32[8,8]{1,0:T(8,128)S(1)}, s32[8,8]{1,0:T(8,128)}, u32[]{:S(2)}) copy-start(s32[8,8]{1,0:T(8,128)} %param.11) | copy-start | bytes 772
  4.8 64.3 %copy-start.2 = (s32[8,8,128]{2,1,0:T(8,128)S(1)}, s32[8,8,128]{2,1,0:T(8,128)}, u32[]{:S(2)}) copy-start(s32[8,8,128]{2,1,0:T(8,128)} %param.8) | copy-start | bytes 98308
  4.8 64.3 %copy-start.3 = (f32[8,8,128]{2,1,0:T(8,128)S(1)}, f32[8,8,128]{2,1,0:T(8,128)}, u32[]{:S(2)}) copy-start(f32[8,8,128]{2,1,0:T(8,128)} %param.9) | copy-start | bytes 98308
  4.8 64.3 %all-to-all-start = ((bf16[128,64,256]{2,1,0:T(8,128)(2,1)}), bf16[128,64,256]{2,1,0:T(8,128)(2,1)}, u32[]{:S(2)}, u32[]{:S(2)}) async-start(bf16[128,64,256]{2,1,0:T(8,128)(2,1)} %bitcast.33), calls=%async_computation | async-start | bytes 8388608 | tf_op jit(solution)/shard_map/all_to_all | solution.py:244
  69.1 38.0 %copy-start.5 = (s32[8,8,9]{2,1,0:T(8,128)S(1)}, s32[8,8,9]{2,1,0:T(8,128)}, u32[]{:S(2)}) copy-start(s32[8,8,9]{2,1,0:T(8,128)} %param.12) | copy-start | bytes 6916
  69.1 38.0 %copy-start.7 = (f32[9]{0:T(128)S(1)}, f32[9]{0:T(128)}, u32[]{:S(2)}) copy-start(f32[9]{0:T(128)} %constant.4.clone) | copy-start | bytes 112
  86.2 8.7 %collective-permute-start.1 = (bf16[8,144,128]{2,1,0:T(8,128)(2,1)S(1)}, bf16[8,144,128]{2,1,0:T(8,128)(2,1)S(1)}, u32[]{:S(2)}, u32[]{:S(2)}) collective-permute-start(bf16[8,144,128]{2,1,0:T(8,128)(2,1)S(1)} %get-tuple-element.11), channel_id=1, source_target_pairs={{0,15},{1,0},{2,1},{3,2},{4,3},{5,4},{6,5},{7,6},{8,7},{9,8},{10,9... | collective-permute-start | bytes 884744 | tf_op jit(solution)/shard_map/ppermute | solution.py:225
  88.1 10.4 %collective-permute-start = (bf16[8,144,128]{2,1,0:T(8,128)(2,1)S(1)}, bf16[8,144,128]{2,1,0:T(8,128)(2,1)S(1)}, u32[]{:S(2)}, u32[]{:S(2)}) collective-permute-start(bf16[8,144,128]{2,1,0:T(8,128)(2,1)S(1)} %get-tuple-element.12), channel_id=1, source_target_pairs={{0,1},{1,2},{2,3},{3,4},{4,5},{5,6},{6,7},{7,8},{8,9},{9,10},{10,1... | collective-permute-start | bytes 884744 | tf_op jit(solution)/shard_map/ppermute | solution.py:225
  98.5 0.7 copy-start
  100.1 8.9 %collective-permute-start.2 = (bf16[10,144,128]{2,1,0:T(8,128)(2,1)}, bf16[10,144,128]{2,1,0:T(8,128)(2,1)S(1)}, u32[]{:S(2)}, u32[]{:S(2)}) collective-permute-start(bf16[10,144,128]{2,1,0:T(8,128)(2,1)} %pad_maximum_fusion.1), channel_id=1, source_target_pairs={{0,16},{16,32},{32,48},{48,64},{64,80},{80,96},{96,112},{1,17},{17... | collective-permute-start | bytes 1105928 | tf_op jit(solution)/shard_map/ppermute | solution.py:225
  105.0 9.0 %collective-permute-start.3 = (bf16[10,144,128]{2,1,0:T(8,128)(2,1)}, bf16[10,144,128]{2,1,0:T(8,128)(2,1)S(1)}, u32[]{:S(2)}, u32[]{:S(2)}) collective-permute-start(bf16[10,144,128]{2,1,0:T(8,128)(2,1)} %pad_maximum_fusion.2), channel_id=1, source_target_pairs={{16,0},{32,16},{48,32},{64,48},{80,64},{96,80},{112,96},{17,1},{33... | collective-permute-start | bytes 1105928 | tf_op jit(solution)/shard_map/ppermute | solution.py:225
  114.1 1.0 copy-start.1

commit v2 on v0

v2 whole, which is shorter than its diff:
```python
import jax
import jax.numpy as jnp
from jax import lax
from jax.experimental import pallas as pl
from jax.experimental.pallas import tpu as pltpu
from jax.sharding import PartitionSpec as P

NS_STEPS = 5
TAPER_WEIGHTS = (0.3, 0.6, 0.3, 0.6, 1.0, 0.6, 0.3, 0.6, 0.3)
INFLATION = 1.1
F32 = jnp.float32
BF16 = jnp.bfloat16
PAD = 16
LANES = 128
AXES = ("mem", "blk")
VMEM_LIMIT = 62 * 1024 * 1024


def select(state, cell, value, root):
    members, _, cells = state.shape
    lat, cols, slots = cell.shape
    blocks = lat * cols
    group = 2 * cols
    pitch = group + 1

    def kernel(x_ref, cell_ref, value_ref, root_ref, xt_ref, gh_ref, first_ref, last_ref, wide, seen, left_ref):
        for k in range(members):
            part = x_ref[k].astype(F32)
            for h in range(cells // LANES):
                wide[h, k * pitch : k * pitch + group, :] = part[:, h * LANES : (h + 1) * LANES]
        ids = lax.broadcasted_iota(jnp.int32, (cells, slots), 0)
        pad_row = lax.broadcasted_iota(jnp.int32, (PAD, slots), 0)
        step = pl.program_id(0)

        def lat_row(half, carry):
            row = 2 * step + half
            means, lefts = [], []
            for j in range(cols):
                b = half * cols + j
                own = jnp.concatenate(
                    [
                        wide[h, pl.ds(b, members, stride=pitch), :].astype(BF16)
                        for h in range(cells // LANES)
                    ],
                    axis=1,
                )
                xt_ref[b] = own
                selector = (ids == cell_ref[row, j : j + 1, :]).astype(BF16)
                obs = jnp.dot(own, selector, preferred_element_type=F32)
                seen[j] = obs
                means.append(jnp.sum(obs, axis=0, keepdims=True) * (1.0 / members))
            for j in range(cols):
                scale = root_ref[row, j : j + 1, :]
                depart = (value_ref[row, j : j + 1, :] - means[j]) * scale
                high = depart.astype(BF16).astype(F32)
                extra = jnp.where(pad_row == 0, high, jnp.where(pad_row == 1, depart - high, 0.0))
                left_ref[j, :members] = ((seen[j] - means[j]) * scale).astype(BF16)
                left_ref[j, members:] = extra.astype(BF16)
            for j in range(cols):
                b = half * cols + j
                gram = lax.dot_general(
                    left_ref[j],
                    left_ref[j, :members],
                    (((1,), (1,)), ((), ())),
                    preferred_element_type=F32,
                )
                gain = gram[members : members + 1] + gram[members + 1 : members + 2]
                upper = gain.astype(BF16).astype(F32)
                tail = jnp.where(pad_row == 0, upper, jnp.where(pad_row == 1, gain - upper, 0.0))
                gram = gram[:members].astype(BF16)
                tail = tail.astype(BF16)
                targets = [gh_ref.at[b]]
                targets += [first_ref.at[half]] if j == 0 else []
                targets += [last_ref.at[half]] if j == cols - 1 else []
                for target in targets:
                    target[:members] = gram
                    target[members:] = tail
            return carry

        lax.fori_loop(0, 2, lat_row, 0)

    whole = pl.BlockSpec(cell.shape, lambda i: (0, 0, 0))
    edge = pl.BlockSpec((2, members + PAD, members), lambda i: (i, 0, 0))
    return pl.pallas_call(
        kernel,
        grid=(blocks // group,),
        in_specs=[
            pl.BlockSpec((members, group, cells), lambda i: (0, i, 0)),
            whole,
            whole,
            whole,
        ],
        out_specs=[
            pl.BlockSpec((group, members, cells), lambda i: (i, 0, 0)),
            pl.BlockSpec((group, members + PAD, members), lambda i: (i, 0, 0)),
            edge,
            edge,
        ],
        out_shape=[
            jax.ShapeDtypeStruct((blocks, members, cells), BF16),
            jax.ShapeDtypeStruct((blocks, members + PAD, members), BF16),
            jax.ShapeDtypeStruct((lat, members + PAD, members), BF16),
            jax.ShapeDtypeStruct((lat, members + PAD, members), BF16),
        ],
        scratch_shapes=[
            pltpu.VMEM((cells // LANES, members * pitch, LANES), F32),
            pltpu.VMEM((cols, members, slots), F32),
            pltpu.VMEM((cols, members + PAD, slots), BF16),
        ],
        compiler_params=pltpu.CompilerParams(vmem_limit_bytes=VMEM_LIMIT),
        cost_estimate=cost(blocks, 0.27),
        name="select",
    )(state, cell, value, root)


def cost(blocks, micros):
    return pl.CostEstimate(
        flops=int(blocks * micros * 1.1e9), bytes_accessed=blocks * 1000, transcendentals=0
    )


def interleave(main, other):
    done = 0
    for i, unit in enumerate(main):
        unit()
        while done < len(other) and done * len(main) < (i + 1) * len(other):
            other[done]()
            done += 1
    for unit in other[done:]:
        unit()


def combine_units(sites, base, gh, weight, cols, members, pq_f, pq_b, bd, norms, gains):
    ident = (
        lax.broadcasted_iota(jnp.int32, (members, members), 0)
        == lax.broadcasted_iota(jnp.int32, (members, members), 1)
    ).astype(F32)

    def unit(j, r, c):
        acc = None
        for n in range(9):
            term = gh[r - base[0] + n // 3, c - base[1] + n % 3].astype(F32)
            term = term * weight[(r * cols + c) * 9 + n]
            acc = term if acc is None else acc + term
        info = acc[:members] + (members - 1) / INFLATION * ident
        gains[r, c] = acc[members : members + 1] + acc[members + 1 : members + 2]
        inv = lax.rsqrt(jnp.sum(jnp.sum(info * info, axis=0, keepdims=True), axis=1, keepdims=True))
        norms[r, c] = inv
        p = info * inv
        third = p * (1.0 / 3.0)
        q = ident - third
        pq_f[j, :members] = p
        pq_b[j, :members] = p.astype(BF16)
        pq_f[j, members:] = q
        pq_b[j, members:] = q.astype(BF16)
        bd[j] = third.astype(BF16)

    return [lambda j=j, r=r, c=c: unit(j, r, c) for j, (r, c) in enumerate(sites)]


def newton_units(count, members, pq_f, pq_b, bd):
    c = members

    def opening(j):
        p = pq_f[j, :c] - jnp.dot(pq_b[j, :c], bd[j], preferred_element_type=F32)
        pq_f[j, :c] = p
        pq_b[j, :c] = p.astype(BF16)

    def product(j, step):
        scale = 1.5 ** (2 * step) / 3.0
        prod = jnp.dot(pq_b[j, c:], pq_b[j, :c], preferred_element_type=F32)
        bd[j] = (prod * scale).astype(BF16)

    def update(j, step):
        start = 0 if step < NS_STEPS - 1 else c
        new = pq_f[j, start:] - jnp.dot(pq_b[j, start:], bd[j], preferred_element_type=F32)
        pq_f[j, start:] = new
        if start == 0:
            pq_b[j] = new.astype(BF16)

    units = [lambda j=j: opening(j) for j in range(count)]
    for step in range(1, NS_STEPS):
        for part in (product, update):
            units += [lambda j=j, step=step, part=part: part(j, step) for j in range(count)]
    return units


def transform_of(j, site, members, pq_f, norms, gains):
    q = pq_f[j, members:] * 1.5**NS_STEPS
    inv = norms[site]
    column = jnp.sum(q * gains[site], axis=1, keepdims=True)
    weights_row = jnp.sum(q * column, axis=0, keepdims=True) * inv
    return (q * jnp.sqrt((members - 1.0) * inv) + weights_row).astype(BF16)


def inner_transforms(gh, weight, sites, first, depth, members, cols):
    c = members
    most = max(map(len, sites))
    total = sum(map(len, sites))

    def kernel(weight_ref, gh_ref, out_ref, held, pq_f, pq_b, bd, sem):
        def fetch(i):
            return pltpu.make_async_copy(gh_ref.at[first + i], held.at[i], sem.at[i])

        for i in range(depth):
            fetch(i).start()
        norms, gains = {}, {}

        def combine(g):
            two = g % 2
            return combine_units(
                sites[g], (first + 1, 1), held, weight_ref, cols, members,
                pq_f.at[two], pq_b.at[two], bd.at[two], norms, gains,
            )

        def finish(g):
            at = sum(map(len, sites[:g]))

            def unit(j, site):
                out_ref[at + j] = transform_of(j, site, members, pq_f.at[g % 2], norms, gains)

            return [lambda j=j, site=site: unit(j, site) for j, site in enumerate(sites[g])]

        for i in range(depth - len(sites) + 1):
            fetch(i).wait()
        interleave(combine(0), [])
        for g in range(len(sites)):
            beside = finish(g - 1) if g else []
            if g + 1 < len(sites):
                fetch(depth - len(sites) + 1 + g).wait()
                beside = beside + combine(g + 1)
            two = g % 2
            units = newton_units(len(sites[g]), members, pq_f.at[two], pq_b.at[two], bd.at[two])
            interleave(units, beside)
        interleave(finish(len(sites) - 1), [])

    return pl.pallas_call(
        kernel,
        in_specs=[pl.BlockSpec(memory_space=pltpu.SMEM), pl.BlockSpec(memory_space=pl.ANY)],
        out_specs=pl.BlockSpec(memory_space=pltpu.VMEM),
        out_shape=jax.ShapeDtypeStruct((total, members, members), BF16),
        scratch_shapes=[
            pltpu.VMEM((depth, cols, members + PAD, members), BF16),
            pltpu.VMEM((2, most, 2 * c, c), F32),
            pltpu.VMEM((2, most, 2 * c, c), BF16),
            pltpu.VMEM((2, most, c, c), BF16),
            pltpu.SemaphoreType.DMA((depth,)),
        ],
        compiler_params=pltpu.CompilerParams(vmem_limit_bytes=VMEM_LIMIT),
        cost_estimate=cost(total, 0.4),
        name="inner_transforms",
    )(weight, gh)


def analyse(weight, gh, west, east, south, north, xt, ready, ready_sites):
    lat, cols, tall, members = gh.shape
    cells = xt.shape[2]
    c = members
    pitch = 2 * cols + 1
    pairs = lat // 2
    site_of = {site: i for ref, sites in enumerate(ready_sites) for i, site in enumerate(sites)}
    array_of = {site: ref for ref, sites in enumerate(ready_sites) for site in sites}
    rim = [[(r, k) for r in range(lat) for k in range(cols) if (r, k) not in site_of and p(r)]
           for p in (lambda r: 2 <= r < lat - 2, lambda r: r < 2, lambda r: r >= lat - 2)]
    most = max(map(len, rim))
    middle = list(range(1, pairs - 1))
    finished = [middle, [0], [pairs - 1]]

    def kernel(*refs):
        weight_ref, gh_ref, west_ref, east_ref, south_ref, north_ref, xt_ref = refs[:7]
        ready_refs = refs[7 : 7 + len(ready)]
        (out_ref, held, states, kept_a, kept_b, pq_f, pq_b, bd, wide, narrow,
         row_sem, state_sem, kept_sem, out_sem) = refs[7 + len(ready) :]
        kept = (kept_a, kept_b)

        def copy(src, dst, sem):
            pltpu.make_async_copy(src, dst, sem).start()

        for r in list(range(1, lat - 1)) + [0, lat - 1]:
            copy(gh_ref.at[r], held.at[r + 1, pl.ds(1, cols)], row_sem.at[r + 1])
            copy(west_ref.at[pl.ds(r, 1)], held.at[r + 1, pl.ds(0, 1)], row_sem.at[r + 1])
            copy(east_ref.at[pl.ds(r, 1)], held.at[r + 1, pl.ds(cols + 1, 1)], row_sem.at[r + 1])
        for src, dst, sem in zip(ready_refs, kept, (0, 1)):
            copy(src, dst, kept_sem.at[sem])
        for pair in middle + [0, pairs - 1]:
            span = pl.ds(pair * 2 * cols, 2 * cols)
            copy(xt_ref.at[span], states.at[span], state_sem.at[pair])
        copy(south_ref, held.at[0], row_sem.at[0])
        copy(north_ref, held.at[lat + 1], row_sem.at[lat + 1])

        def rows_in(*which):
            for r in which:
                pltpu.make_async_copy(held.at[r], held.at[r], row_sem.at[r]).wait()

        def states_in(*which):
            for pair in which:
                span = pl.ds(pair * 2 * cols, 2 * cols)
                pltpu.make_async_copy(states.at[span], states.at[span], state_sem.at[pair]).wait()

        norms, gains = {}, {}

        def combine(g):
            two = g % 2
            return combine_units(
                rim[g], (0, 0), held, weight_ref, cols, members,
                pq_f.at[two], pq_b.at[two], bd.at[two], norms, gains,
            )

        def apply(r, k, transform):
            ones = jnp.full((PAD, members), 1.0 / members, BF16)
            rest = 1.0 - jnp.sum(transform.astype(F32), axis=1, keepdims=True)
            left = jnp.concatenate([transform, ones], axis=0)
            out = jnp.dot(left, states[r * cols + k], preferred_element_type=F32)
            out = out[:members] + rest * out[members : members + 1]
            for h in range(cells // LANES):
                wide[r // 2, h, pl.ds(r % 2 * cols + k, members, stride=pitch), :] = (
                    out[:, h * LANES : (h + 1) * LANES]
                )

        def inner(which):
            sites = [site for site in site_of if site[0] // 2 in which]
            return [
                lambda s=s: apply(*s, kept[array_of[s]][site_of[s]]) for s in sites
            ]

        def finish(g):
            return [
                lambda j=j, s=s: apply(
                    *s, transform_of(j, s, members, pq_f.at[g % 2], norms, gains)
                )
                for j, s in enumerate(rim[g])
            ]

        def sent(pair):
            return pltpu.make_async_copy(
                narrow.at[pair], out_ref.at[:, pl.ds(pair * 2 * cols, 2 * cols)],
                out_sem.at[pair],
            )

        def convert(pair):
            def unit(start):
                for k in range(start, start + members // 8):
                    for h in range(cells // LANES):
                        part = wide[pair, h, k * pitch : k * pitch + 2 * cols, :]
                        narrow[pair, k, :, h * LANES : (h + 1) * LANES] = part.astype(BF16)

            units = [lambda k=k: unit(k) for k in range(0, members, members // 8)]
            return units + [lambda: sent(pair).start()]

        def newton(g):
            two = g % 2
            return newton_units(len(rim[g]), members, pq_f.at[two], pq_b.at[two], bd.at[two])

        rows_in(*range(2, lat))
        interleave(combine(0), [])
        for i in range(len(ready)):
            pltpu.make_async_copy(kept[i], kept[i], kept_sem.at[i]).wait()
        states_in(*middle)
        rows_in(0, 1)
        interleave(newton(0), combine(1) + inner(middle))
        rows_in(lat, lat + 1)
        states_in(0, pairs - 1)
        beside = finish(0) + combine(2)
        for pair in middle:
            beside = beside + convert(pair)
        interleave(newton(1), beside + inner([0]))
        interleave(newton(2), finish(1) + convert(0) + inner([pairs - 1]))
        interleave(finish(2) + convert(pairs - 1), [])
        for pair in range(pairs):
            sent(pair).wait()

    any_spec = pl.BlockSpec(memory_space=pl.ANY)
    return pl.pallas_call(
        kernel,
        in_specs=[pl.BlockSpec(memory_space=pltpu.SMEM)] + [any_spec] * (6 + len(ready)),
        out_specs=any_spec,
        out_shape=jax.ShapeDtypeStruct((members, lat * cols, cells), BF16),
        scratch_shapes=[
            pltpu.VMEM((lat + 2, cols + 2, tall, members), BF16),
            pltpu.VMEM(xt.shape, BF16),
            pltpu.VMEM(ready[0].shape, BF16),
            pltpu.VMEM(ready[1].shape, BF16),
            pltpu.VMEM((2, most, 2 * c, c), F32),
            pltpu.VMEM((2, most, 2 * c, c), BF16),
            pltpu.VMEM((2, most, c, c), BF16),
            pltpu.VMEM((pairs, cells // LANES, members * pitch, LANES), F32),
            pltpu.VMEM((pairs, members, 2 * cols, cells), BF16),
            pltpu.SemaphoreType.DMA((lat + 2,)),
            pltpu.SemaphoreType.DMA((pairs,)),
            pltpu.SemaphoreType.DMA((2,)),
            pltpu.SemaphoreType.DMA((pairs,)),
        ],
        compiler_params=pltpu.CompilerParams(vmem_limit_bytes=VMEM_LIMIT),
        cost_estimate=cost(lat * cols, 0.25),
        name="analyse",
    )(weight, gh, west, east, south, north, xt, *ready)


def shift(value, axis, step, wrap):
    count = lax.axis_size(axis)
    pairs = [(i, (i + step) % count) for i in range(count) if wrap or 0 <= i + step < count]
    return lax.ppermute(value, axis, pairs)


def shards(members, obs_cell, obs_value, obs_rinv, obs_count, loc_pattern):
    mem_count = lax.axis_size("mem")
    blk_count = lax.axis_size("blk")
    devices = mem_count * blk_count
    lat_all, lon_all, cells = members.shape[1:]
    lat, lon = lat_all // mem_count, lon_all // blk_count
    slots = obs_cell.shape[2]

    live = lax.broadcasted_iota(jnp.int32, obs_rinv.shape, 2) < obs_count[:, :, None]
    root = jnp.sqrt(jnp.where(live, obs_rinv, 0.0))
    weight = (
        jnp.asarray(TAPER_WEIGHTS, F32) * loc_pattern.astype(F32)
    ).reshape(lat * lon * 9)

    tiled = members.reshape(mem_count, lat, blk_count, lon, cells).transpose(0, 2, 1, 3, 4)
    arrived = lax.all_to_all(
        tiled.reshape(devices, lat * lon, cells), AXES, split_axis=0, concat_axis=0, tiled=True
    )
    xt, gh, first, last = select(arrived, obs_cell, obs_value, root)
    gh = gh.reshape(lat, lon, *gh.shape[1:])
    west = shift(last, "blk", 1, True)
    east = shift(first, "blk", -1, True)
    half = lat // 2
    inner = [
        [[(r, c) for c in range(1, lon - 1)] for r in rows]
        for rows in (range(1, half), range(half, lat - 1))
    ]
    ready = [
        inner_transforms(gh, weight, sites, start, half + 1, devices, lon)
        for sites, start in zip(inner, (0, half - 1))
    ]

    def full_row(r):
        return jnp.concatenate([west[r][None], gh[r], east[r][None]], axis=0)

    south = shift(full_row(lat - 1), "mem", 1, False)
    north = shift(full_row(0), "mem", -1, False)
    result = analyse(
        weight, gh, west, east, south, north, xt, ready, [sum(sites, []) for sites in inner]
    )
    back = lax.all_to_all(result, AXES, split_axis=0, concat_axis=0, tiled=True)
    back = back.reshape(mem_count, blk_count, lat, lon, cells).transpose(0, 2, 1, 3, 4)
    return back.reshape(1, lat_all, lon_all, cells)


def solution(mesh):
    in_specs = (
        P(AXES, None, None, None),
        P("mem", "blk", None),
        P("mem", "blk", None),
        P("mem", "blk", None),
        P("mem", "blk"),
        P("mem", "blk", None),
    )
    out_specs = P(AXES, None, None, None)
    return jax.shard_map(shards, mesh=mesh, in_specs=in_specs, out_specs=out_specs, check_vma=False)
```

time: 636 us -> 181 us (0.28); the launches traced: 625 us -> 180 us
  matrix products: 216 us -> 0 us
  blocking collectives: 170 us -> 57.7 us
  local copies, waits for them, and re-layouts: 96.5 us -> 9.96 us
  Pallas kernels: 0 us -> 38.9 us
  other arithmetic: 32.6 us -> 0.8 us
  loops' own time: 31.3 us -> 0 us
  waiting for transfers between devices: 63.3 us -> 50.9 us
  starting transfers between devices: 14.9 us -> 21.8 us
    dot_general x153 -> x0, matrix products: 216 us -> none  [the longest x8 58.9 us: analyse_row(): gain_in = jnp.einsum('bkp,bp->bk', scaled, departure, precision=highest)]
    all_to_all x3 -> x1, blocking collectives: 170 us -> 57.7 us  [shards(): back = lax.all_to_all(result, AXES, split_axis=0, concat_axis=0, tiled=True)]
    slice x16 -> x3, local copies, waits for them, and re-layouts: 44.7 us -> 1.11 us  [full_row(): return jnp.concatenate([west[r][None], gh[r], east[r][None]], axis=0)]
    pallas_call x0 -> x4, Pallas kernels: none -> 38.9 us  [the longest x2 17.4 us: inner_transforms(): pl.pallas_call(kernel, in_specs=[pl.BlockSpec(memory_space=pltpu.SMEM), p...]
    another operation x1 -> x0, loops' own time: 31.3 us -> none  [shards(): lax.map(one_row, (jnp.arange(lat_rows, dtype=jnp.int32), loc_pattern, sta...]
    all_to_all x4 -> x0, local copies, waits for them, and re-layouts: 13.6 us -> none  [the longest x1 5.12 us: shards(): lax.all_to_all(lax.all_to_all(members, 'mem', split_axis=1, concat_axis=0...]
    mul x25 -> x1, other arithmetic: 10.6 us -> 0.01 us  [shards(): jnp.asarray(TAPER_WEIGHTS, F32) * loc_pattern.astype(F32)]
    while x40 -> x0, local copies, waits for them, and re-layouts: 10.6 us -> none
  transfers between devices with their start and end apart: 5 -> 5, of which waited for: 4 -> 1; matrix products, arithmetic and copies ran while one was open for 1% -> 1% of each run, Pallas kernels for 0% -> 10%
where the time goes in v2:
time: 181 us; the launch traced here: 180 us
  blocking collectives  57.7 us (32%)
  waiting for transfers between devices  50.9 us (28%)
  Pallas kernels  38.9 us (21%)
  starting transfers between devices  21.8 us (12%)
  local copies, waits for them, and re-layouts  9.96 us (6%)
    all_to_all x1, blocking collectives, shards(): back = lax.all_to_all(result, AXES, split_axis=0, concat_axis=0, tiled=True)  57.7 us
    all_to_all x1, waiting for transfers between devices, shards(): lax.all_to_all(tiled.reshape(devices, lat * lon, cells), AXES, split_axis...  50.9 us
    pallas_call x2, Pallas kernels, inner_transforms(): pl.pallas_call(kernel, in_specs=[pl.BlockSpec(memory_space=pltpu.SMEM), p...  17.4 us
    pallas_call x1, Pallas kernels, analyse(): pl.pallas_call(kernel, in_specs=[pl.BlockSpec(memory_space=pltpu.SMEM)] +...  13.1 us
    all_to_all x1, starting transfers between devices, shards(): lax.all_to_all(tiled.reshape(devices, lat * lon, cells), AXES, split_axis...  12 us
    ppermute x4, starting transfers between devices, shift(): return lax.ppermute(value, axis, pairs)  9.85 us
    pallas_call x1, Pallas kernels, select(): pl.pallas_call(kernel, grid=(blocks // group,), in_specs=[pl.BlockSpec((m...  8.36 us
    reshape x1, local copies, waits for them, and re-layouts, shards(): members.reshape(mem_count, lat, blk_count, lon, cells)  4.79 us
  transfers between devices with their start and end apart: 5, of which 1 were waited for; matrix products, arithmetic and copies ran while one was open for 1% of the time, Pallas kernels for 10%

profile of v2, /device:TPU:1, one launch (start us, length us, event | category | flops | bytes accessed | tf_op | source)
XLA Modules:
  0.0 180.3 jit_solution(434148442915129027)
XLA Ops:
  0.0 4.8 %copy.8 = bf16[8,8,16,8,256]{4,3,1,2,0:T(8,128)(2,1)} copy(bf16[8,8,16,8,256]{4,3,2,1,0:T(8,128)(2,1)} %bitcast.11) | data formatting | bytes 8388608 | tf_op jit(solution)/shard_map/reshape | solution.py:419
  4.8 0.0 copy-start
  4.8 0.0 copy-start.5
  4.8 0.0 copy-start.1
  4.8 0.0 copy-start.4
  4.8 12.0 %all-to-all-start = ((bf16[128,64,256]{2,1,0:T(8,128)(2,1)}), bf16[128,64,256]{2,1,0:T(8,128)(2,1)}, u32[]{:S(2)}, u32[]{:S(2)}) async-start(bf16[128,64,256]{2,1,0:T(8,128)(2,1)} %bitcast.9), calls=%async_computation | async-start | bytes 8388608 | tf_op jit(solution)/shard_map/all_to_all | solution.py:420
  16.8 0.0 copy-done
  16.8 0.0 copy-done.5
  16.8 0.7 reshape.24.weight_ref.refs_0_
  17.5 0.0 copy-done.1
  17.5 0.0 copy-done.4
  17.5 0.7 select_sqrt_fusion.root_ref
  18.2 50.9 %all-to-all-done.x_ref = bf16[128,64,256]{2,1,0:T(8,128)(2,1)} async-done(((bf16[128,64,256]{2,1,0:T(8,128)(2,1)}), bf16[128,64,256]{2,1,0:T(8,128)(2,1)}, u32[]{:S(2)}, u32[]{:S(2)}) %all-to-all-start) | async-done | bytes 4194336 | tf_op jit(solution)/shard_map/all_to_all | solution.py:420
  69.1 8.4 %select.1 = (bf16[64,128,256]{2,1,0:T(8,128)(2,1)}, bf16[64,144,128]{2,1,0:T(8,128)(2,1)}, bf16[8,144,128]{2,1,0:T(8,128)(2,1)}, bf16[8,144,128]{2,1,0:T(8,128)(2,1)}) custom-call(bf16[128,64,256]{2,1,0:T(8,128)(2,1)} %all-to-all-done.x_ref, s32[8,8,128]{2,1,0:T(8,128)} %cell_ref.1, f32[8,8,128]{2,1,0:T(8,128)} %value_ref.1, ...), custom_call_target="tpu_custom_call" | custom-call | flops 19008000000 | bytes 64000 | tf_op jit(solution)/shard_map/select/pallas_call | solution.py:84
  77.4 0.2 collective-permute-start
  77.7 4.6 %collective-permute-start.1 = (bf16[8,144,128]{2,1,0:T(8,128)(2,1)}, bf16[8,144,128]{2,1,0:T(8,128)(2,1)S(1)}, u32[]{:S(2)}, u32[]{:S(2)}) collective-permute-start(bf16[8,144,128]{2,1,0:T(8,128)(2,1)} %get-tuple-element.11), channel_id=1, source_target_pairs={{0,15},{1,0},{2,1},{3,2},{4,3},{5,4},{6,5},{7,6},{8,7},{9,8},{10,9... | collective-permute-start | bytes 884744 | tf_op jit(solution)/shard_map/ppermute | solution.py:402
  82.3 8.7 %inner_transforms.3.refs_8_ = bf16[18,128,128]{2,1,0:T(8,128)(2,1)} custom-call(f32[576]{0:T(1024)} %reshape.24.weight_ref.refs_0_, bf16[8,8,144,128]{3,2,1,0:T(8,128)(2,1)} %bitcast.12), custom_call_target="tpu_custom_call" | custom-call | flops 7920000000 | bytes 18000 | tf_op jit(solution)/shard_map/inner_transforms/pallas_call | solution.py:237
  91.0 1.1 fusion
  92.1 0.0 collective-permute-done.refs_2_
  92.1 0.0 copy-start.2
  92.1 0.0 collective-permute-done.1.refs_3_
  92.2 0.0 copy-start.3
  92.2 0.1 pad_maximum_fusion
  92.2 2.9 %collective-permute-start.2 = (bf16[10,144,128]{2,1,0:T(8,128)(2,1)S(1)}, bf16[10,144,128]{2,1,0:T(8,128)(2,1)S(1)}, u32[]{:S(2)}, u32[]{:S(2)}) collective-permute-start(bf16[10,144,128]{2,1,0:T(8,128)(2,1)S(1)} %pad_maximum_fusion), channel_id=1, source_target_pairs={{0,16},{16,32},{32,48},{48,64},{64,80},{80,96},{96,112},{1,17},{17... | collective-permute-start | bytes 1105928 | tf_op jit(solution)/shard_map/ppermute | solution.py:402
  95.2 0.1 pad_maximum_fusion.1
  95.2 2.1 %collective-permute-start.3 = (bf16[10,144,128]{2,1,0:T(8,128)(2,1)S(1)}, bf16[10,144,128]{2,1,0:T(8,128)(2,1)}, u32[]{:S(2)}, u32[]{:S(2)}) collective-permute-start(bf16[10,144,128]{2,1,0:T(8,128)(2,1)S(1)} %pad_maximum_fusion.1), channel_id=1, source_target_pairs={{16,0},{32,16},{48,32},{64,48},{80,64},{96,80},{112,96},{17,1},{33... | collective-permute-start | bytes 1105928 | tf_op jit(solution)/shard_map/ppermute | solution.py:402
  97.3 8.7 %inner_transforms.2.refs_7_ = bf16[18,128,128]{2,1,0:T(8,128)(2,1)} custom-call(f32[576]{0:T(1024)} %reshape.24.weight_ref.refs_0_, bf16[8,8,144,128]{3,2,1,0:T(8,128)(2,1)} %bitcast.13), custom_call_target="tpu_custom_call" | custom-call | flops 7920000000 | bytes 18000 | tf_op jit(solution)/shard_map/inner_transforms/pallas_call | solution.py:237
  106.0 0.0 copy-done.2
  106.0 0.0 copy-done.3
  106.1 0.0 collective-permute-done.2.refs_4_
  106.1 0.0 copy-start.6
  106.1 0.0 collective-permute-done.3.refs_5_
  106.1 0.7 copy-done.6
  106.8 13.1 %analyse.1 = bf16[128,64,256]{2,1,0:T(8,128)(2,1)} custom-call(f32[576]{0:T(1024)} %reshape.24.weight_ref.refs_0_, bf16[8,8,144,128]{3,2,1,0:T(8,128)(2,1)} %bitcast.14, bf16[8,144,128]{2,1,0:T(8,128)(2,1)} %copy-done.2, bf16[8,144,128]{2,1,0:T(8,128)(2,1)} %copy-done.3, bf16[10,144,128]{2,1,0:T(8,128)(2,1)} %copy-done.6, ...), custom_call_target="tpu_custom_call" | custom-call | flops 17600000000 | bytes 64000 | tf_op jit(solution)/shard_map/analyse/pallas_call | solution.py:373
  119.9 57.7 %all_to_all.10 = bf16[128,64,256]{2,1,0:T(8,128)(2,1)S(1)} all-to-all(bf16[128,64,256]{2,1,0:T(8,128)(2,1)} %analyse.1), channel_id=1, replica_groups=mesh['mem'=8,'blk'=16] {'mem','blk'}, dimensions={0} | all-to-all | bytes 8388608 | tf_op jit(solution)/shard_map/all_to_all | solution.py:445
  177.7 2.6 %copy.9 = bf16[8,8,16,8,256]{4,3,2,1,0:T(8,128)(2,1)} copy(bf16[8,8,16,8,256]{4,3,1,2,0:T(8,128)(2,1)S(1)} %bitcast.10) | data formatting | bytes 8388608 | tf_op jit(solution)/shard_map/transpose | solution.py:446
  (3 shorter events, 0.0 us)
Async XLA Ops:
  4.8 12.0 %copy-start = (s32[8,8,9]{2,1,0:T(8,128)S(1)}, s32[8,8,9]{2,1,0:T(8,128)}, u32[]{:S(2)}) copy-start(s32[8,8,9]{2,1,0:T(8,128)} %param.12) | copy-start | bytes 6916
  4.8 12.0 %copy-start.5 = (f32[9]{0:T(128)S(1)}, f32[9]{0:T(128)}, u32[]{:S(2)}) copy-start(f32[9]{0:T(128)} %constant.4.clone) | copy-start | bytes 112
  4.8 12.7 %copy-start.1 = (f32[8,8,128]{2,1,0:T(8,128)S(1)}, f32[8,8,128]{2,1,0:T(8,128)}, u32[]{:S(2)}) copy-start(f32[8,8,128]{2,1,0:T(8,128)} %param.10) | copy-start | bytes 98308
  4.8 12.7 %copy-start.4 = (s32[8,8]{1,0:T(8,128)S(1)}, s32[8,8]{1,0:T(8,128)}, u32[]{:S(2)}) copy-start(s32[8,8]{1,0:T(8,128)} %param.11) | copy-start | bytes 772
  4.8 64.3 %all-to-all-start = ((bf16[128,64,256]{2,1,0:T(8,128)(2,1)}), bf16[128,64,256]{2,1,0:T(8,128)(2,1)}, u32[]{:S(2)}, u32[]{:S(2)}) async-start(bf16[128,64,256]{2,1,0:T(8,128)(2,1)} %bitcast.9), calls=%async_computation | async-start | bytes 8388608 | tf_op jit(solution)/shard_map/all_to_all | solution.py:420
  77.4 14.7 %collective-permute-start = (bf16[8,144,128]{2,1,0:T(8,128)(2,1)}, bf16[8,144,128]{2,1,0:T(8,128)(2,1)S(1)}, u32[]{:S(2)}, u32[]{:S(2)}) collective-permute-start(bf16[8,144,128]{2,1,0:T(8,128)(2,1)} %get-tuple-element.10), channel_id=1, source_target_pairs={{0,1},{1,2},{2,3},{3,4},{4,5},{5,6},{6,7},{7,8},{8,9},{9,10},{10,1... | collective-permute-start | bytes 884744 | tf_op jit(solution)/shard_map/ppermute | solution.py:402
  77.7 14.5 %collective-permute-start.1 = (bf16[8,144,128]{2,1,0:T(8,128)(2,1)}, bf16[8,144,128]{2,1,0:T(8,128)(2,1)S(1)}, u32[]{:S(2)}, u32[]{:S(2)}) collective-permute-start(bf16[8,144,128]{2,1,0:T(8,128)(2,1)} %get-tuple-element.11), channel_id=1, source_target_pairs={{0,15},{1,0},{2,1},{3,2},{4,3},{5,4},{6,5},{7,6},{8,7},{9,8},{10,9... | collective-permute-start | bytes 884744 | tf_op jit(solution)/shard_map/ppermute | solution.py:402
  92.1 13.9 %copy-start.2 = (bf16[8,144,128]{2,1,0:T(8,128)(2,1)}, bf16[8,144,128]{2,1,0:T(8,128)(2,1)S(1)}, u32[]{:S(2)}) copy-start(bf16[8,144,128]{2,1,0:T(8,128)(2,1)S(1)} %collective-permute-done.refs_2_) | copy-start | bytes 884740
  92.2 13.9 %copy-start.3 = (bf16[8,144,128]{2,1,0:T(8,128)(2,1)}, bf16[8,144,128]{2,1,0:T(8,128)(2,1)S(1)}, u32[]{:S(2)}) copy-start(bf16[8,144,128]{2,1,0:T(8,128)(2,1)S(1)} %collective-permute-done.1.refs_3_) | copy-start | bytes 884740
  92.2 13.8 %collective-permute-start.2 = (bf16[10,144,128]{2,1,0:T(8,128)(2,1)S(1)}, bf16[10,144,128]{2,1,0:T(8,128)(2,1)S(1)}, u32[]{:S(2)}, u32[]{:S(2)}) collective-permute-start(bf16[10,144,128]{2,1,0:T(8,128)(2,1)S(1)} %pad_maximum_fusion), channel_id=1, source_target_pairs={{0,16},{16,32},{32,48},{48,64},{64,80},{80,96},{96,112},{1,17},{17... | collective-permute-start | bytes 1105928 | tf_op jit(solution)/shard_map/ppermute | solution.py:402
  95.2 10.9 %collective-permute-start.3 = (bf16[10,144,128]{2,1,0:T(8,128)(2,1)S(1)}, bf16[10,144,128]{2,1,0:T(8,128)(2,1)}, u32[]{:S(2)}, u32[]{:S(2)}) collective-permute-start(bf16[10,144,128]{2,1,0:T(8,128)(2,1)S(1)} %pad_maximum_fusion.1), channel_id=1, source_target_pairs={{16,0},{32,16},{48,32},{64,48},{80,64},{96,80},{112,96},{17,1},{33... | collective-permute-start | bytes 1105928 | tf_op jit(solution)/shard_map/ppermute | solution.py:402
  106.1 0.8 copy-start.6

commit v3 on v2

--- a/solution.py
+++ b/solution.py
@@ -16,20 +16,21 @@
 VMEM_LIMIT = 62 * 1024 * 1024
 
 
-def select(state, cell, value, root):
+def select(state, cell, value, rinv, live):
     members, _, cells = state.shape
     lat, cols, slots = cell.shape
     blocks = lat * cols
     group = 2 * cols
     pitch = group + 1
 
-    def kernel(x_ref, cell_ref, value_ref, root_ref, xt_ref, gh_ref, first_ref, last_ref, wide, seen, left_ref):
+    def kernel(x_ref, cell_ref, value_ref, rinv_ref, live_ref, xt_ref, gh_ref, first_ref, last_ref, wide, seen, left_ref):
         for k in range(members):
             part = x_ref[k].astype(F32)
             for h in range(cells // LANES):
                 wide[h, k * pitch : k * pitch + group, :] = part[:, h * LANES : (h + 1) * LANES]
         ids = lax.broadcasted_iota(jnp.int32, (cells, slots), 0)
         pad_row = lax.broadcasted_iota(jnp.int32, (PAD, slots), 0)
+        slot = lax.broadcasted_iota(jnp.int32, (1, slots), 1)
         step = pl.program_id(0)
 
         def lat_row(half, carry):
@@ -50,7 +51,8 @@
                 seen[j] = obs
                 means.append(jnp.sum(obs, axis=0, keepdims=True) * (1.0 / members))
             for j in range(cols):
-                scale = root_ref[row, j : j + 1, :]
+                weight = jnp.where(slot < live_ref[row, j], rinv_ref[row, j : j + 1, :], 0.0)
+                scale = jnp.sqrt(weight)
                 depart = (value_ref[row, j : j + 1, :] - means[j]) * scale
                 high = depart.astype(BF16).astype(F32)
                 extra = jnp.where(pad_row == 0, high, jnp.where(pad_row == 1, depart - high, 0.0))
@@ -89,6 +91,7 @@
             whole,
             whole,
             whole,
+            pl.BlockSpec(memory_space=pltpu.SMEM),
         ],
         out_specs=[
             pl.BlockSpec((group, members, cells), lambda i: (i, 0, 0)),
@@ -110,7 +113,7 @@
         compiler_params=pltpu.CompilerParams(vmem_limit_bytes=VMEM_LIMIT),
         cost_estimate=cost(blocks, 0.27),
         name="select",
-    )(state, cell, value, root)
+    )(state, cell, value, rinv, live)
 
 
 def cost(blocks, micros):
@@ -130,7 +133,7 @@
         unit()
 
 
-def combine_units(sites, base, gh, weight, cols, members, pq_f, pq_b, bd, norms, gains):
+def combine_units(sites, base, gh, pattern, cols, members, pq_f, pq_b, bd, norms, gains):
     ident = (
         lax.broadcasted_iota(jnp.int32, (members, members), 0)
         == lax.broadcasted_iota(jnp.int32, (members, members), 1)
@@ -140,7 +143,7 @@
         acc = None
         for n in range(9):
             term = gh[r - base[0] + n // 3, c - base[1] + n % 3].astype(F32)
-            term = term * weight[(r * cols + c) * 9 + n]
+            term = term * (TAPER_WEIGHTS[n] * pattern[r, c, n].astype(F32))
             acc = term if acc is None else acc + term
         info = acc[:members] + (members - 1) / INFLATION * ident
         gains[r, c] = acc[members : members + 1] + acc[members + 1 : members + 2]
@@ -193,12 +196,12 @@
     return (q * jnp.sqrt((members - 1.0) * inv) + weights_row).astype(BF16)
 
 
-def inner_transforms(gh, weight, sites, first, depth, members, cols):
+def inner_transforms(gh, pattern, sites, first, depth, members, cols):
     c = members
     most = max(map(len, sites))
     total = sum(map(len, sites))
 
-    def kernel(weight_ref, gh_ref, out_ref, held, pq_f, pq_b, bd, sem):
+    def kernel(pattern_ref, gh_ref, out_ref, held, pq_f, pq_b, bd, sem):
         def fetch(i):
             return pltpu.make_async_copy(gh_ref.at[first + i], held.at[i], sem.at[i])
 
@@ -209,7 +212,7 @@
         def combine(g):
             two = g % 2
             return combine_units(
-                sites[g], (first + 1, 1), held, weight_ref, cols, members,
+                sites[g], (first + 1, 1), held, pattern_ref, cols, members,
                 pq_f.at[two], pq_b.at[two], bd.at[two], norms, gains,
             )
 
@@ -249,60 +252,60 @@
         compiler_params=pltpu.CompilerParams(vmem_limit_bytes=VMEM_LIMIT),
         cost_estimate=cost(total, 0.4),
         name="inner_transforms",
-    )(weight, gh)
-
-
-def analyse(weight, gh, west, east, south, north, xt, ready, ready_sites):
+    )(pattern, gh)
+
+
+def analyse(pattern, gh, west, east, beyond, xt, pairs, groups, ready, ready_sites):
     lat, cols, tall, members = gh.shape
     cells = xt.shape[2]
     c = members
     pitch = 2 * cols + 1
-    pairs = lat // 2
-    site_of = {site: i for ref, sites in enumerate(ready_sites) for i, site in enumerate(sites)}
-    array_of = {site: ref for ref, sites in enumerate(ready_sites) for site in sites}
-    rim = [[(r, k) for r in range(lat) for k in range(cols) if (r, k) not in site_of and p(r)]
-           for p in (lambda r: 2 <= r < lat - 2, lambda r: r < 2, lambda r: r >= lat - 2)]
-    most = max(map(len, rim))
-    middle = list(range(1, pairs - 1))
-    finished = [middle, [0], [pairs - 1]]
+    most = max(map(len, groups))
+    span = 2 * cols
+    last_of = {p: max(g for g, sites in enumerate(groups) for r, _ in sites if r // 2 == p)
+               for p in pairs}
+    slot = {p: i for i, p in enumerate(pairs)}
+    needed = [sorted({r + a for r, _ in sites for a in range(3)}) for sites in groups]
+    fresh = [[r for r in rows if all(r not in old for old in needed[:g])]
+             for g, rows in enumerate(needed)]
+    sources = [pattern, gh, west, east, xt, *beyond, *ready]
+    starts = [sum(map(len, ready_sites[:i])) for i in range(len(ready_sites))]
 
     def kernel(*refs):
-        weight_ref, gh_ref, west_ref, east_ref, south_ref, north_ref, xt_ref = refs[:7]
-        ready_refs = refs[7 : 7 + len(ready)]
-        (out_ref, held, states, kept_a, kept_b, pq_f, pq_b, bd, wide, narrow,
-         row_sem, state_sem, kept_sem, out_sem) = refs[7 + len(ready) :]
-        kept = (kept_a, kept_b)
+        pattern_ref, gh_ref, west_ref, east_ref, xt_ref = refs[:5]
+        beyond_refs = refs[5 : 5 + len(beyond)]
+        ready_refs = refs[5 + len(beyond) : len(sources)]
+        (out_ref, held, states, kept, pq_f, pq_b, bd, wide, narrow,
+         row_sem, state_sem, kept_sem, out_sem) = refs[len(sources) :]
 
         def copy(src, dst, sem):
             pltpu.make_async_copy(src, dst, sem).start()
 
-        for r in list(range(1, lat - 1)) + [0, lat - 1]:
-            copy(gh_ref.at[r], held.at[r + 1, pl.ds(1, cols)], row_sem.at[r + 1])
-            copy(west_ref.at[pl.ds(r, 1)], held.at[r + 1, pl.ds(0, 1)], row_sem.at[r + 1])
-            copy(east_ref.at[pl.ds(r, 1)], held.at[r + 1, pl.ds(cols + 1, 1)], row_sem.at[r + 1])
-        for src, dst, sem in zip(ready_refs, kept, (0, 1)):
-            copy(src, dst, kept_sem.at[sem])
-        for pair in middle + [0, pairs - 1]:
-            span = pl.ds(pair * 2 * cols, 2 * cols)
-            copy(xt_ref.at[span], states.at[span], state_sem.at[pair])
-        copy(south_ref, held.at[0], row_sem.at[0])
-        copy(north_ref, held.at[lat + 1], row_sem.at[lat + 1])
-
-        def rows_in(*which):
-            for r in which:
+        for g, rows in enumerate(fresh):
+            for r in rows:
+                if r in (0, lat + 1):
+                    copy(beyond_refs[r // (lat + 1)], held.at[r], row_sem.at[r])
+                    continue
+                copy(gh_ref.at[r - 1], held.at[r, pl.ds(1, cols)], row_sem.at[r])
+                copy(west_ref.at[pl.ds(r - 1, 1)], held.at[r, pl.ds(0, 1)], row_sem.at[r])
+                copy(east_ref.at[pl.ds(r - 1, 1)], held.at[r, pl.ds(cols + 1, 1)], row_sem.at[r])
+            if g == 0:
+                for i, ref in enumerate(ready_refs):
+                    copy(ref, kept.at[pl.ds(starts[i], ref.shape[0])], kept_sem.at[i])
+                for p in pairs:
+                    copy(xt_ref.at[pl.ds(p * span, span)], states.at[slot[p]],
+                         state_sem.at[slot[p]])
+
+        def rows_in(g):
+            for r in fresh[g]:
                 pltpu.make_async_copy(held.at[r], held.at[r], row_sem.at[r]).wait()
-
-        def states_in(*which):
-            for pair in which:
-                span = pl.ds(pair * 2 * cols, 2 * cols)
-                pltpu.make_async_copy(states.at[span], states.at[span], state_sem.at[pair]).wait()
 
         norms, gains = {}, {}
 
         def combine(g):
             two = g % 2
             return combine_units(
-                rim[g], (0, 0), held, weight_ref, cols, members,
+                groups[g], (0, 0), held, pattern_ref, cols, members,
                 pq_f.at[two], pq_b.at[two], bd.at[two], norms, gains,
             )
 
@@ -310,90 +313,90 @@
             ones = jnp.full((PAD, members), 1.0 / members, BF16)
             rest = 1.0 - jnp.sum(transform.astype(F32), axis=1, keepdims=True)
             left = jnp.concatenate([transform, ones], axis=0)
-            out = jnp.dot(left, states[r * cols + k], preferred_element_type=F32)
+            at = r % 2 * cols + k
+            out = jnp.dot(left, states[slot[r // 2], at], preferred_element_type=F32)
             out = out[:members] + rest * out[members : members + 1]
             for h in range(cells // LANES):
-                wide[r // 2, h, pl.ds(r % 2 * cols + k, members, stride=pitch), :] = (
+                wide[slot[r // 2], h, pl.ds(at, members, stride=pitch), :] = (
                     out[:, h * LANES : (h + 1) * LANES]
                 )
 
-        def inner(which):
-            sites = [site for site in site_of if site[0] // 2 in which]
-            return [
-                lambda s=s: apply(*s, kept[array_of[s]][site_of[s]]) for s in sites
-            ]
-
         def finish(g):
-            return [
+            units = [
                 lambda j=j, s=s: apply(
                     *s, transform_of(j, s, members, pq_f.at[g % 2], norms, gains)
                 )
-                for j, s in enumerate(rim[g])
+                for j, s in enumerate(groups[g])
             ]
-
-        def sent(pair):
+            for p in pairs:
+                if last_of[p] == g:
+                    units += convert(slot[p])
+            return units
+
+        def sent(i):
             return pltpu.make_async_copy(
-                narrow.at[pair], out_ref.at[:, pl.ds(pair * 2 * cols, 2 * cols)],
-                out_sem.at[pair],
+                narrow.at[i], out_ref.at[:, pl.ds(i * span, span)], out_sem.at[i]
             )
 
-        def convert(pair):
+        def convert(i):
             def unit(start):
                 for k in range(start, start + members // 8):
                     for h in range(cells // LANES):
-                        part = wide[pair, h, k * pitch : k * pitch + 2 * cols, :]
-                        narrow[pair, k, :, h * LANES : (h + 1) * LANES] = part.astype(BF16)
+                        part = wide[i, h, k * pitch : k * pitch + span, :]
+                        narrow[i, k, :, h * LANES : (h + 1) * LANES] = part.astype(BF16)
 
             units = [lambda k=k: unit(k) for k in range(0, members, members // 8)]
-            return units + [lambda: sent(pair).start()]
-
-        def newton(g):
+            return units + [lambda: sent(i).start()]
+
+        rows_in(0)
+        interleave(combine(0), [])
+        for i, ref in enumerate(ready_refs):
+            part = kept.at[pl.ds(starts[i], ref.shape[0])]
+            pltpu.make_async_copy(part, part, kept_sem.at[i]).wait()
+        for p in pairs:
+            i = slot[p]
+            pltpu.make_async_copy(states.at[i], states.at[i], state_sem.at[i]).wait()
+        for g in range(len(groups)):
+            beside = finish(g - 1) if g else []
+            beside = beside + [
+                lambda i=i, s=s: apply(*s, kept[i])
+                for i, s in enumerate(ready_sites[g], starts[g])
+            ]
+            if g + 1 < len(groups):
+                rows_in(g + 1)
+                beside = beside + combine(g + 1)
             two = g % 2
-            return newton_units(len(rim[g]), members, pq_f.at[two], pq_b.at[two], bd.at[two])
-
-        rows_in(*range(2, lat))
-        interleave(combine(0), [])
-        for i in range(len(ready)):
-            pltpu.make_async_copy(kept[i], kept[i], kept_sem.at[i]).wait()
-        states_in(*middle)
-        rows_in(0, 1)
-        interleave(newton(0), combine(1) + inner(middle))
-        rows_in(lat, lat + 1)
-        states_in(0, pairs - 1)
-        beside = finish(0) + combine(2)
-        for pair in middle:
-            beside = beside + convert(pair)
-        interleave(newton(1), beside + inner([0]))
-        interleave(newton(2), finish(1) + convert(0) + inner([pairs - 1]))
-        interleave(finish(2) + convert(pairs - 1), [])
-        for pair in range(pairs):
-            sent(pair).wait()
+            units = newton_units(len(groups[g]), members, pq_f.at[two], pq_b.at[two], bd.at[two])
+            interleave(units, beside)
+        interleave(finish(len(groups) - 1), [])
+        for p in pairs:
+            sent(slot[p]).wait()
 
     any_spec = pl.BlockSpec(memory_space=pl.ANY)
+    count = len(pairs)
     return pl.pallas_call(
         kernel,
-        in_specs=[pl.BlockSpec(memory_space=pltpu.SMEM)] + [any_spec] * (6 + len(ready)),
+        in_specs=[pl.BlockSpec(memory_space=pltpu.SMEM)] + [any_spec] * (len(sources) - 1),
         out_specs=any_spec,
-        out_shape=jax.ShapeDtypeStruct((members, lat * cols, cells), BF16),
+        out_shape=jax.ShapeDtypeStruct((members, count * span, cells), BF16),
         scratch_shapes=[
             pltpu.VMEM((lat + 2, cols + 2, tall, members), BF16),
-            pltpu.VMEM(xt.shape, BF16),
-            pltpu.VMEM(ready[0].shape, BF16),
-            pltpu.VMEM(ready[1].shape, BF16),
+            pltpu.VMEM((count, span, members, cells), BF16),
+            pltpu.VMEM((sum(map(len, ready_sites)), members, members), BF16),
             pltpu.VMEM((2, most, 2 * c, c), F32),
             pltpu.VMEM((2, most, 2 * c, c), BF16),
             pltpu.VMEM((2, most, c, c), BF16),
-            pltpu.VMEM((pairs, cells // LANES, members * pitch, LANES), F32),
-            pltpu.VMEM((pairs, members, 2 * cols, cells), BF16),
+            pltpu.VMEM((count, cells // LANES, members * pitch, LANES), F32),
+            pltpu.VMEM((count, members, span, cells), BF16),
             pltpu.SemaphoreType.DMA((lat + 2,)),
-            pltpu.SemaphoreType.DMA((pairs,)),
-            pltpu.SemaphoreType.DMA((2,)),
-            pltpu.SemaphoreType.DMA((pairs,)),
+            pltpu.SemaphoreType.DMA((count,)),
+            pltpu.SemaphoreType.DMA((len(ready),)),
+            pltpu.SemaphoreType.DMA((count,)),
         ],
         compiler_params=pltpu.CompilerParams(vmem_limit_bytes=VMEM_LIMIT),
-        cost_estimate=cost(lat * cols, 0.25),
+        cost_estimate=cost(count * span, 0.35),
         name="analyse",
-    )(weight, gh, west, east, south, north, xt, *ready)
+    )(*sources)
 
 
 def shift(value, axis, step, wrap):
@@ -410,28 +413,26 @@
     lat, lon = lat_all // mem_count, lon_all // blk_count
     slots = obs_cell.shape[2]
 
-    live = lax.broadcasted_iota(jnp.int32, obs_rinv.shape, 2) < obs_count[:, :, None]
-    root = jnp.sqrt(jnp.where(live, obs_rinv, 0.0))
-    weight = (
-        jnp.asarray(TAPER_WEIGHTS, F32) * loc_pattern.astype(F32)
-    ).reshape(lat * lon * 9)
-
     tiled = members.reshape(mem_count, lat, blk_count, lon, cells).transpose(0, 2, 1, 3, 4)
     arrived = lax.all_to_all(
         tiled.reshape(devices, lat * lon, cells), AXES, split_axis=0, concat_axis=0, tiled=True
     )
-    xt, gh, first, last = select(arrived, obs_cell, obs_value, root)
+    xt, gh, first, last = select(arrived, obs_cell, obs_value, obs_rinv, obs_count)
     gh = gh.reshape(lat, lon, *gh.shape[1:])
     west = shift(last, "blk", 1, True)
     east = shift(first, "blk", -1, True)
     half = lat // 2
     inner = [
-        [[(r, c) for c in range(1, lon - 1)] for r in rows]
+        [(r, c) for r in rows for c in range(1, lon - 1)]
         for rows in (range(1, half), range(half, lat - 1))
     ]
     ready = [
-        inner_transforms(gh, weight, sites, start, half + 1, devices, lon)
+        inner_transforms(gh, loc_pattern, [sites], start, half + 1, devices, lon)
         for sites, start in zip(inner, (0, half - 1))
+    ]
+    rim = [
+        [(r, c) for r in rows for c in range(lon) if (r, c) not in inner[0] + inner[1]]
+        for rows in (range(half), range(half, lat))
     ]
 
     def full_row(r):
@@ -440,7 +441,7 @@
     south = shift(full_row(lat - 1), "mem", 1, False)
     north = shift(full_row(0), "mem", -1, False)
     result = analyse(
-        weight, gh, west, east, south, north, xt, ready, [sum(sites, []) for sites in inner]
+        loc_pattern, gh, west, east, [south, north], xt, tuple(range(half)), rim, ready, inner
     )
     back = lax.all_to_all(result, AXES, split_axis=0, concat_axis=0, tiled=True)
     back = back.reshape(mem_count, blk_count, lat, lon, cells).transpose(0, 2, 1, 3, 4)

time: 181 us -> 177 us (0.978)
  blocking collectives: 57.7 us -> 123 us
  waiting for transfers between devices: 50.9 us -> 0.01 us
  starting transfers between devices: 21.8 us -> 9.86 us
  Pallas kernels: 38.9 us -> 35.6 us
  local copies, waits for them, and re-layouts: 9.96 us -> 7.18 us
    all_to_all x0 -> x1, blocking collectives: none -> 64.1 us  [shards(): lax.all_to_all(tiled.reshape(devices, lat * lon, cells), AXES, split_axis...]
    all_to_all x1 -> x0, waiting for transfers between devices: 50.9 us -> none  [shards(): lax.all_to_all(tiled.reshape(devices, lat * lon, cells), AXES, split_axis...]
    all_to_all x1 -> x0, starting transfers between devices: 12 us -> none  [shards(): lax.all_to_all(tiled.reshape(devices, lat * lon, cells), AXES, split_axis...]
    pallas_call x2, Pallas kernels: 17.4 us -> 14.2 us  [inner_transforms(): pl.pallas_call(kernel, in_specs=[pl.BlockSpec(memory_space=pltpu.SMEM), p...]
    reshape x1, local copies, waits for them, and re-layouts: 4.79 us -> 2.76 us  [shards(): members.reshape(mem_count, lat, blk_count, lon, cells)]
  transfers between devices with their start and end apart: 5 -> 4, of which waited for: 1 -> 0; matrix products, arithmetic and copies ran while one was open for 1% -> 1% of each run, Pallas kernels for 10% -> 8%
where the time goes in v3:
time: 177 us; the launch traced here: 176 us
  blocking collectives  123 us (69%)
  Pallas kernels  35.6 us (20%)
  starting transfers between devices  9.86 us (6%)
  local copies, waits for them, and re-layouts  7.18 us (4%)
    all_to_all x1, blocking collectives, shards(): lax.all_to_all(tiled.reshape(devices, lat * lon, cells), AXES, split_axis...  64.1 us
    all_to_all x1, blocking collectives, shards(): back = lax.all_to_all(result, AXES, split_axis=0, concat_axis=0, tiled=True)  59.4 us
    pallas_call x2, Pallas kernels, inner_transforms(): pl.pallas_call(kernel, in_specs=[pl.BlockSpec(memory_space=pltpu.SMEM), p...  14.2 us
    pallas_call x1, Pallas kernels, analyse(): pl.pallas_call(kernel, in_specs=[pl.BlockSpec(memory_space=pltpu.SMEM)] +...  13 us
    ppermute x4, starting transfers between devices, shift(): return lax.ppermute(value, axis, pairs)  9.86 us
    pallas_call x1, Pallas kernels, select(): pl.pallas_call(kernel, grid=(blocks // group,), in_specs=[pl.BlockSpec((m...  8.4 us
  transfers between devices with their start and end apart: 4, of which 0 were waited for; matrix products, arithmetic and copies ran while one was open for 1% of the time, Pallas kernels for 8%

profile of v3, /device:TPU:1, one launch (start us, length us, event | category | flops | bytes accessed | tf_op | source)
XLA Modules:
  0.0 176.3 jit_solution(13784078099414513867)
XLA Ops:
  0.0 2.8 %copy.7 = bf16[8,8,16,8,256]{4,3,1,2,0:T(8,128)(2,1)S(1)} copy(bf16[8,8,16,8,256]{4,3,2,1,0:T(8,128)(2,1)} %bitcast.11) | data formatting | bytes 8388608 | tf_op jit(solution)/shard_map/reshape | solution.py:416
  2.8 64.1 %all_to_all.10.x_ref = bf16[128,64,256]{2,1,0:T(8,128)(2,1)} all-to-all(bf16[128,64,256]{2,1,0:T(8,128)(2,1)S(1)} %bitcast.10), channel_id=1, replica_groups=mesh['mem'=8,'blk'=16] {'mem','blk'}, dimensions={0} | all-to-all | bytes 8388608 | tf_op jit(solution)/shard_map/all_to_all | solution.py:417
  66.8 8.4 %select.1 = (bf16[64,128,256]{2,1,0:T(8,128)(2,1)}, bf16[64,144,128]{2,1,0:T(8,128)(2,1)}, bf16[8,144,128]{2,1,0:T(8,128)(2,1)}, bf16[8,144,128]{2,1,0:T(8,128)(2,1)}) custom-call(bf16[128,64,256]{2,1,0:T(8,128)(2,1)} %all_to_all.10.x_ref, s32[8,8,128]{2,1,0:T(8,128)} %cell_ref.1, f32[8,8,128]{2,1,0:T(8,128)} %value_ref.1, f32[8,8,128]{2,1,0:T(8,128)} %rinv_ref.1, ...), custom_call_target="tpu_custom_call" | custom-call | flops 19008000000 | bytes 64000 | tf_op jit(solution)/shard_map/select/pallas_call | solution.py:86
  75.2 0.2 collective-permute-start
  75.5 4.6 %collective-permute-start.1 = (bf16[8,144,128]{2,1,0:T(8,128)(2,1)}, bf16[8,144,128]{2,1,0:T(8,128)(2,1)S(1)}, u32[]{:S(2)}, u32[]{:S(2)}) collective-permute-start(bf16[8,144,128]{2,1,0:T(8,128)(2,1)} %get-tuple-element.11), channel_id=1, source_target_pairs={{0,15},{1,0},{2,1},{3,2},{4,3},{5,4},{6,5},{7,6},{8,7},{9,8},{10,9... | collective-permute-start | bytes 884744 | tf_op jit(solution)/shard_map/ppermute | solution.py:405
  80.1 7.1 %inner_transforms.3.refs_8_ = bf16[18,128,128]{2,1,0:T(8,128)(2,1)} custom-call(s32[8,8,9]{2,1,0:T(8,128)} %refs_0_.1, bf16[8,8,144,128]{3,2,1,0:T(8,128)(2,1)} %bitcast.12), custom_call_target="tpu_custom_call" | custom-call | flops 7920000000 | bytes 18000 | tf_op jit(solution)/shard_map/inner_transforms/pallas_call | solution.py:240
  87.2 1.1 fusion
  88.3 0.0 collective-permute-done.refs_2_
  88.3 0.0 copy-start
  88.3 0.0 collective-permute-done.1.refs_3_
  88.3 0.0 copy-start.1
  88.3 0.1 pad_maximum_fusion
  88.4 2.9 %collective-permute-start.2 = (bf16[10,144,128]{2,1,0:T(8,128)(2,1)S(1)}, bf16[10,144,128]{2,1,0:T(8,128)(2,1)S(1)}, u32[]{:S(2)}, u32[]{:S(2)}) collective-permute-start(bf16[10,144,128]{2,1,0:T(8,128)(2,1)S(1)} %pad_maximum_fusion), channel_id=1, source_target_pairs={{0,16},{16,32},{32,48},{48,64},{64,80},{80,96},{96,112},{1,17},{17... | collective-permute-start | bytes 1105928 | tf_op jit(solution)/shard_map/ppermute | solution.py:405
  91.3 0.1 pad_maximum_fusion.1
  91.4 2.1 %collective-permute-start.3 = (bf16[10,144,128]{2,1,0:T(8,128)(2,1)S(1)}, bf16[10,144,128]{2,1,0:T(8,128)(2,1)}, u32[]{:S(2)}, u32[]{:S(2)}) collective-permute-start(bf16[10,144,128]{2,1,0:T(8,128)(2,1)S(1)} %pad_maximum_fusion.1), channel_id=1, source_target_pairs={{16,0},{32,16},{48,32},{64,48},{80,64},{96,80},{112,96},{17,1},{33... | collective-permute-start | bytes 1105928 | tf_op jit(solution)/shard_map/ppermute | solution.py:405
  93.5 7.1 %inner_transforms.2.refs_7_ = bf16[18,128,128]{2,1,0:T(8,128)(2,1)} custom-call(s32[8,8,9]{2,1,0:T(8,128)} %refs_0_.1, bf16[8,8,144,128]{3,2,1,0:T(8,128)(2,1)} %bitcast.13), custom_call_target="tpu_custom_call" | custom-call | flops 7920000000 | bytes 18000 | tf_op jit(solution)/shard_map/inner_transforms/pallas_call | solution.py:240
  100.6 0.0 copy-done
  100.6 0.0 copy-done.1
  100.6 0.0 collective-permute-done.2.refs_5_
  100.6 0.0 copy-start.2
  100.6 0.0 collective-permute-done.3.refs_6_
  100.6 0.7 copy-done.2
  101.4 13.0 %analyse.1 = bf16[128,64,256]{2,1,0:T(8,128)(2,1)} custom-call(s32[8,8,9]{2,1,0:T(8,128)} %refs_0_.1, bf16[8,8,144,128]{3,2,1,0:T(8,128)(2,1)} %bitcast.14, bf16[8,144,128]{2,1,0:T(8,128)(2,1)} %copy-done, bf16[8,144,128]{2,1,0:T(8,128)(2,1)} %copy-done.1, bf16[64,128,256]{2,1,0:T(8,128)(2,1)} %get-tuple-element.12.refs_4_, bf16[10,144,128]{2,1,0:T(8,128)(2,1)} %copy-done.2, ...), custom_call_target="tpu_custom_call" | custom-call | flops 24640000000 | bytes 64000 | tf_op jit(solution)/shard_map/analyse/pallas_call | solution.py:377
  114.4 59.4 %all_to_all.11 = bf16[128,64,256]{2,1,0:T(8,128)(2,1)S(1)} all-to-all(bf16[128,64,256]{2,1,0:T(8,128)(2,1)} %analyse.1), channel_id=1, replica_groups=mesh['mem'=8,'blk'=16] {'mem','blk'}, dimensions={0} | all-to-all | bytes 8388608 | tf_op jit(solution)/shard_map/all_to_all | solution.py:446
  173.7 2.6 %copy.8 = bf16[8,8,16,8,256]{4,3,2,1,0:T(8,128)(2,1)} copy(bf16[8,8,16,8,256]{4,3,1,2,0:T(8,128)(2,1)S(1)} %bitcast.9) | data formatting | bytes 8388608 | tf_op jit(solution)/shard_map/transpose | solution.py:447
  (2 shorter events, 0.0 us)
Async XLA Ops:
  75.2 13.0 %collective-permute-start = (bf16[8,144,128]{2,1,0:T(8,128)(2,1)}, bf16[8,144,128]{2,1,0:T(8,128)(2,1)S(1)}, u32[]{:S(2)}, u32[]{:S(2)}) collective-permute-start(bf16[8,144,128]{2,1,0:T(8,128)(2,1)} %get-tuple-element.10), channel_id=1, source_target_pairs={{0,1},{1,2},{2,3},{3,4},{4,5},{5,6},{6,7},{7,8},{8,9},{9,10},{10,1... | collective-permute-start | bytes 884744 | tf_op jit(solution)/shard_map/ppermute | solution.py:405
  75.5 12.8 %collective-permute-start.1 = (bf16[8,144,128]{2,1,0:T(8,128)(2,1)}, bf16[8,144,128]{2,1,0:T(8,128)(2,1)S(1)}, u32[]{:S(2)}, u32[]{:S(2)}) collective-permute-start(bf16[8,144,128]{2,1,0:T(8,128)(2,1)} %get-tuple-element.11), channel_id=1, source_target_pairs={{0,15},{1,0},{2,1},{3,2},{4,3},{5,4},{6,5},{7,6},{8,7},{9,8},{10,9... | collective-permute-start | bytes 884744 | tf_op jit(solution)/shard_map/ppermute | solution.py:405
  88.3 12.3 %copy-start = (bf16[8,144,128]{2,1,0:T(8,128)(2,1)}, bf16[8,144,128]{2,1,0:T(8,128)(2,1)S(1)}, u32[]{:S(2)}) copy-start(bf16[8,144,128]{2,1,0:T(8,128)(2,1)S(1)} %collective-permute-done.refs_2_) | copy-start | bytes 884740
  88.3 12.3 %copy-start.1 = (bf16[8,144,128]{2,1,0:T(8,128)(2,1)}, bf16[8,144,128]{2,1,0:T(8,128)(2,1)S(1)}, u32[]{:S(2)}) copy-start(bf16[8,144,128]{2,1,0:T(8,128)(2,1)S(1)} %collective-permute-done.1.refs_3_) | copy-start | bytes 884740
  88.4 12.2 %collective-permute-start.2 = (bf16[10,144,128]{2,1,0:T(8,128)(2,1)S(1)}, bf16[10,144,128]{2,1,0:T(8,128)(2,1)S(1)}, u32[]{:S(2)}, u32[]{:S(2)}) collective-permute-start(bf16[10,144,128]{2,1,0:T(8,128)(2,1)S(1)} %pad_maximum_fusion), channel_id=1, source_target_pairs={{0,16},{16,32},{32,48},{48,64},{64,80},{80,96},{96,112},{1,17},{17... | collective-permute-start | bytes 1105928 | tf_op jit(solution)/shard_map/ppermute | solution.py:405
  91.4 9.2 %collective-permute-start.3 = (bf16[10,144,128]{2,1,0:T(8,128)(2,1)S(1)}, bf16[10,144,128]{2,1,0:T(8,128)(2,1)}, u32[]{:S(2)}, u32[]{:S(2)}) collective-permute-start(bf16[10,144,128]{2,1,0:T(8,128)(2,1)S(1)} %pad_maximum_fusion.1), channel_id=1, source_target_pairs={{16,0},{32,16},{48,32},{64,48},{80,64},{96,80},{112,96},{17,1},{33... | collective-permute-start | bytes 1105928 | tf_op jit(solution)/shard_map/ppermute | solution.py:405
  100.6 0.7 copy-start.2

commit v4 on v3

--- a/solution.py
+++ b/solution.py
@@ -33,53 +33,51 @@
         slot = lax.broadcasted_iota(jnp.int32, (1, slots), 1)
         step = pl.program_id(0)
 
-        def lat_row(half, carry):
+        means = []
+        for b in range(2 * cols):
+            half, j = divmod(b, cols)
             row = 2 * step + half
-            means, lefts = [], []
-            for j in range(cols):
-                b = half * cols + j
-                own = jnp.concatenate(
-                    [
-                        wide[h, pl.ds(b, members, stride=pitch), :].astype(BF16)
-                        for h in range(cells // LANES)
-                    ],
-                    axis=1,
-                )
-                xt_ref[b] = own
-                selector = (ids == cell_ref[row, j : j + 1, :]).astype(BF16)
-                obs = jnp.dot(own, selector, preferred_element_type=F32)
-                seen[j] = obs
-                means.append(jnp.sum(obs, axis=0, keepdims=True) * (1.0 / members))
-            for j in range(cols):
-                weight = jnp.where(slot < live_ref[row, j], rinv_ref[row, j : j + 1, :], 0.0)
-                scale = jnp.sqrt(weight)
-                depart = (value_ref[row, j : j + 1, :] - means[j]) * scale
-                high = depart.astype(BF16).astype(F32)
-                extra = jnp.where(pad_row == 0, high, jnp.where(pad_row == 1, depart - high, 0.0))
-                left_ref[j, :members] = ((seen[j] - means[j]) * scale).astype(BF16)
-                left_ref[j, members:] = extra.astype(BF16)
-            for j in range(cols):
-                b = half * cols + j
-                gram = lax.dot_general(
-                    left_ref[j],
-                    left_ref[j, :members],
-                    (((1,), (1,)), ((), ())),
-                    preferred_element_type=F32,
-                )
-                gain = gram[members : members + 1] + gram[members + 1 : members + 2]
-                upper = gain.astype(BF16).astype(F32)
-                tail = jnp.where(pad_row == 0, upper, jnp.where(pad_row == 1, gain - upper, 0.0))
-                gram = gram[:members].astype(BF16)
-                tail = tail.astype(BF16)
-                targets = [gh_ref.at[b]]
-                targets += [first_ref.at[half]] if j == 0 else []
-                targets += [last_ref.at[half]] if j == cols - 1 else []
-                for target in targets:
-                    target[:members] = gram
-                    target[members:] = tail
-            return carry
-
-        lax.fori_loop(0, 2, lat_row, 0)
+            own = jnp.concatenate(
+                [
+                    wide[h, pl.ds(b, members, stride=pitch), :].astype(BF16)
+                    for h in range(cells // LANES)
+                ],
+                axis=1,
+            )
+            xt_ref[b] = own
+            selector = (ids == cell_ref[row, j : j + 1, :]).astype(BF16)
+            obs = jnp.dot(own, selector, preferred_element_type=F32)
+            seen[b] = obs
+            means.append(jnp.sum(obs, axis=0, keepdims=True) * (1.0 / members))
+        for b in range(2 * cols):
+            half, j = divmod(b, cols)
+            row = 2 * step + half
+            weight = jnp.where(slot < live_ref[row, j], rinv_ref[row, j : j + 1, :], 0.0)
+            scale = jnp.sqrt(weight)
+            depart = (value_ref[row, j : j + 1, :] - means[b]) * scale
+            high = depart.astype(BF16).astype(F32)
+            extra = jnp.where(pad_row == 0, high, jnp.where(pad_row == 1, depart - high, 0.0))
+            left_ref[b, :members] = ((seen[b] - means[b]) * scale).astype(BF16)
+            left_ref[b, members:] = extra.astype(BF16)
+        for b in range(2 * cols):
+            half, j = divmod(b, cols)
+            gram = lax.dot_general(
+                left_ref[b],
+                left_ref[b, :members],
+                (((1,), (1,)), ((), ())),
+                preferred_element_type=F32,
+            )
+            gain = gram[members : members + 1] + gram[members + 1 : members + 2]
+            upper = gain.astype(BF16).astype(F32)
+            tail = jnp.where(pad_row == 0, upper, jnp.where(pad_row == 1, gain - upper, 0.0))
+            gram = gram[:members].astype(BF16)
+            tail = tail.astype(BF16)
+            targets = [gh_ref.at[b]]
+            targets += [first_ref.at[half]] if j == 0 else []
+            targets += [last_ref.at[half]] if j == cols - 1 else []
+            for target in targets:
+                target[:members] = gram
+                target[members:] = tail
 
     whole = pl.BlockSpec(cell.shape, lambda i: (0, 0, 0))
     edge = pl.BlockSpec((2, members + PAD, members), lambda i: (i, 0, 0))
@@ -107,8 +105,8 @@
         ],
         scratch_shapes=[
             pltpu.VMEM((cells // LANES, members * pitch, LANES), F32),
-            pltpu.VMEM((cols, members, slots), F32),
-            pltpu.VMEM((cols, members + PAD, slots), BF16),
+            pltpu.VMEM((2 * cols, members, slots), F32),
+            pltpu.VMEM((2 * cols, members + PAD, slots), BF16),
         ],
         compiler_params=pltpu.CompilerParams(vmem_limit_bytes=VMEM_LIMIT),
         cost_estimate=cost(blocks, 0.27),
@@ -143,7 +141,7 @@
         acc = None
         for n in range(9):
             term = gh[r - base[0] + n // 3, c - base[1] + n % 3].astype(F32)
-            term = term * (TAPER_WEIGHTS[n] * pattern[r, c, n].astype(F32))
+            term = term * (TAPER_WEIGHTS[n] * pattern[r, c : c + 1, n : n + 1].astype(F32))
             acc = term if acc is None else acc + term
         info = acc[:members] + (members - 1) / INFLATION * ident
         gains[r, c] = acc[members : members + 1] + acc[members + 1 : members + 2]
@@ -239,7 +237,7 @@
 
     return pl.pallas_call(
         kernel,
-        in_specs=[pl.BlockSpec(memory_space=pltpu.SMEM), pl.BlockSpec(memory_space=pl.ANY)],
+        in_specs=[pl.BlockSpec(memory_space=pltpu.VMEM), pl.BlockSpec(memory_space=pl.ANY)],
         out_specs=pl.BlockSpec(memory_space=pltpu.VMEM),
         out_shape=jax.ShapeDtypeStruct((total, members, members), BF16),
         scratch_shapes=[
@@ -357,11 +355,11 @@
             i = slot[p]
             pltpu.make_async_copy(states.at[i], states.at[i], state_sem.at[i]).wait()
         for g in range(len(groups)):
-            beside = finish(g - 1) if g else []
-            beside = beside + [
+            beside = [
                 lambda i=i, s=s: apply(*s, kept[i])
                 for i, s in enumerate(ready_sites[g], starts[g])
             ]
+            beside = beside + (finish(g - 1) if g else [])
             if g + 1 < len(groups):
                 rows_in(g + 1)
                 beside = beside + combine(g + 1)
@@ -376,7 +374,7 @@
     count = len(pairs)
     return pl.pallas_call(
         kernel,
-        in_specs=[pl.BlockSpec(memory_space=pltpu.SMEM)] + [any_spec] * (len(sources) - 1),
+        in_specs=[pl.BlockSpec(memory_space=pltpu.VMEM)] + [any_spec] * (len(sources) - 1),
         out_specs=any_spec,
         out_shape=jax.ShapeDtypeStruct((members, count * span, cells), BF16),
         scratch_shapes=[
@@ -432,7 +430,7 @@
     ]
     rim = [
         [(r, c) for r in rows for c in range(lon) if (r, c) not in inner[0] + inner[1]]
-        for rows in (range(half), range(half, lat))
+        for rows in ((0, 1, lat - 2, lat - 1), range(2, lat - 2))
     ]
 
     def full_row(r):

time: 177 us -> 175 us (0.989)
  Pallas kernels: 35.6 us -> 33.1 us
where the time goes in v4:
time: 175 us; the launch traced here: 174 us
  blocking collectives  124 us (71%)
  Pallas kernels  33.1 us (19%)
  starting transfers between devices  9.82 us (6%)
  local copies, waits for them, and re-layouts  7.18 us (4%)
    all_to_all x1, blocking collectives, shards(): lax.all_to_all(tiled.reshape(devices, lat * lon, cells), AXES, split_axis...  64.1 us
    all_to_all x1, blocking collectives, shards(): back = lax.all_to_all(result, AXES, split_axis=0, concat_axis=0, tiled=True)  59.6 us
    pallas_call x2, Pallas kernels, inner_transforms(): pl.pallas_call(kernel, in_specs=[pl.BlockSpec(memory_space=pltpu.VMEM), p...  13.6 us
    pallas_call x1, Pallas kernels, analyse(): pl.pallas_call(kernel, in_specs=[pl.BlockSpec(memory_space=pltpu.VMEM)] +...  12.6 us
    ppermute x4, starting transfers between devices, shift(): return lax.ppermute(value, axis, pairs)  9.82 us
    pallas_call x1, Pallas kernels, select(): pl.pallas_call(kernel, grid=(blocks // group,), in_specs=[pl.BlockSpec((m...  6.92 us
  transfers between devices with their start and end apart: 4, of which 0 were waited for; matrix products, arithmetic and copies ran while one was open for 1% of the time, Pallas kernels for 8%

profile of v4, /device:TPU:1, one launch (start us, length us, event | category | flops | bytes accessed | tf_op | source)
XLA Modules:
  0.0 174.1 jit_solution(4184060012084663275)
XLA Ops:
  0.0 2.8 %copy.7 = bf16[8,8,16,8,256]{4,3,1,2,0:T(8,128)(2,1)S(1)} copy(bf16[8,8,16,8,256]{4,3,2,1,0:T(8,128)(2,1)} %bitcast.11) | data formatting | bytes 8388608 | tf_op jit(solution)/shard_map/reshape | solution.py:414
  2.8 64.1 %all_to_all.10.x_ref = bf16[128,64,256]{2,1,0:T(8,128)(2,1)} all-to-all(bf16[128,64,256]{2,1,0:T(8,128)(2,1)S(1)} %bitcast.10), channel_id=1, replica_groups=mesh['mem'=8,'blk'=16] {'mem','blk'}, dimensions={0} | all-to-all | bytes 8388608 | tf_op jit(solution)/shard_map/all_to_all | solution.py:415
  66.8 6.9 %select.1 = (bf16[64,128,256]{2,1,0:T(8,128)(2,1)}, bf16[64,144,128]{2,1,0:T(8,128)(2,1)}, bf16[8,144,128]{2,1,0:T(8,128)(2,1)}, bf16[8,144,128]{2,1,0:T(8,128)(2,1)}) custom-call(bf16[128,64,256]{2,1,0:T(8,128)(2,1)} %all_to_all.10.x_ref, s32[8,8,128]{2,1,0:T(8,128)} %cell_ref.1, f32[8,8,128]{2,1,0:T(8,128)} %value_ref.1, f32[8,8,128]{2,1,0:T(8,128)} %rinv_ref.1, ...), custom_call_target="tpu_custom_call" | custom-call | flops 19008000000 | bytes 64000 | tf_op jit(solution)/shard_map/select/pallas_call | solution.py:84
  73.8 0.2 collective-permute-start
  74.0 4.6 %collective-permute-start.1 = (bf16[8,144,128]{2,1,0:T(8,128)(2,1)}, bf16[8,144,128]{2,1,0:T(8,128)(2,1)S(1)}, u32[]{:S(2)}, u32[]{:S(2)}) collective-permute-start(bf16[8,144,128]{2,1,0:T(8,128)(2,1)} %get-tuple-element.11), channel_id=1, source_target_pairs={{0,15},{1,0},{2,1},{3,2},{4,3},{5,4},{6,5},{7,6},{8,7},{9,8},{10,9... | collective-permute-start | bytes 884744 | tf_op jit(solution)/shard_map/ppermute | solution.py:403
  78.5 6.8 %inner_transforms.3.refs_8_ = bf16[18,128,128]{2,1,0:T(8,128)(2,1)} custom-call(s32[8,8,9]{2,1,0:T(8,128)} %refs_0_.1, bf16[8,8,144,128]{3,2,1,0:T(8,128)(2,1)} %bitcast.12), custom_call_target="tpu_custom_call" | custom-call | flops 7920000000 | bytes 18000 | tf_op jit(solution)/shard_map/inner_transforms/pallas_call | solution.py:238
  85.4 1.1 fusion
  86.5 0.0 collective-permute-done.refs_2_
  86.5 0.0 copy-start
  86.5 0.0 collective-permute-done.1.refs_3_
  86.5 0.0 copy-start.1
  86.5 0.1 pad_maximum_fusion
  86.6 2.9 %collective-permute-start.2 = (bf16[10,144,128]{2,1,0:T(8,128)(2,1)S(1)}, bf16[10,144,128]{2,1,0:T(8,128)(2,1)S(1)}, u32[]{:S(2)}, u32[]{:S(2)}) collective-permute-start(bf16[10,144,128]{2,1,0:T(8,128)(2,1)S(1)} %pad_maximum_fusion), channel_id=1, source_target_pairs={{0,16},{16,32},{32,48},{48,64},{64,80},{80,96},{96,112},{1,17},{17... | collective-permute-start | bytes 1105928 | tf_op jit(solution)/shard_map/ppermute | solution.py:403
  89.5 0.1 pad_maximum_fusion.1
  89.6 2.1 %collective-permute-start.3 = (bf16[10,144,128]{2,1,0:T(8,128)(2,1)S(1)}, bf16[10,144,128]{2,1,0:T(8,128)(2,1)}, u32[]{:S(2)}, u32[]{:S(2)}) collective-permute-start(bf16[10,144,128]{2,1,0:T(8,128)(2,1)S(1)} %pad_maximum_fusion.1), channel_id=1, source_target_pairs={{16,0},{32,16},{48,32},{64,48},{80,64},{96,80},{112,96},{17,1},{33... | collective-permute-start | bytes 1105928 | tf_op jit(solution)/shard_map/ppermute | solution.py:403
  91.7 6.8 %inner_transforms.2.refs_7_ = bf16[18,128,128]{2,1,0:T(8,128)(2,1)} custom-call(s32[8,8,9]{2,1,0:T(8,128)} %refs_0_.1, bf16[8,8,144,128]{3,2,1,0:T(8,128)(2,1)} %bitcast.13), custom_call_target="tpu_custom_call" | custom-call | flops 7920000000 | bytes 18000 | tf_op jit(solution)/shard_map/inner_transforms/pallas_call | solution.py:238
  98.5 0.0 copy-done
  98.5 0.0 copy-done.1
  98.5 0.0 collective-permute-done.2.refs_5_
  98.5 0.0 copy-start.2
  98.5 0.0 collective-permute-done.3.refs_6_
  98.5 0.7 copy-done.2
  99.3 12.6 %analyse.1 = bf16[128,64,256]{2,1,0:T(8,128)(2,1)} custom-call(s32[8,8,9]{2,1,0:T(8,128)} %refs_0_.1, bf16[8,8,144,128]{3,2,1,0:T(8,128)(2,1)} %bitcast.14, bf16[8,144,128]{2,1,0:T(8,128)(2,1)} %copy-done, bf16[8,144,128]{2,1,0:T(8,128)(2,1)} %copy-done.1, bf16[64,128,256]{2,1,0:T(8,128)(2,1)} %get-tuple-element.12.refs_4_, bf16[10,144,128]{2,1,0:T(8,128)(2,1)} %copy-done.2, ...), custom_call_target="tpu_custom_call" | custom-call | flops 24640000000 | bytes 64000 | tf_op jit(solution)/shard_map/analyse/pallas_call | solution.py:375
  111.9 59.6 %all_to_all.11 = bf16[128,64,256]{2,1,0:T(8,128)(2,1)S(1)} all-to-all(bf16[128,64,256]{2,1,0:T(8,128)(2,1)} %analyse.1), channel_id=1, replica_groups=mesh['mem'=8,'blk'=16] {'mem','blk'}, dimensions={0} | all-to-all | bytes 8388608 | tf_op jit(solution)/shard_map/all_to_all | solution.py:444
  171.5 2.6 %copy.8 = bf16[8,8,16,8,256]{4,3,2,1,0:T(8,128)(2,1)} copy(bf16[8,8,16,8,256]{4,3,1,2,0:T(8,128)(2,1)S(1)} %bitcast.9) | data formatting | bytes 8388608 | tf_op jit(solution)/shard_map/transpose | solution.py:445
  (2 shorter events, 0.0 us)
Async XLA Ops:
  73.8 12.7 %collective-permute-start = (bf16[8,144,128]{2,1,0:T(8,128)(2,1)}, bf16[8,144,128]{2,1,0:T(8,128)(2,1)S(1)}, u32[]{:S(2)}, u32[]{:S(2)}) collective-permute-start(bf16[8,144,128]{2,1,0:T(8,128)(2,1)} %get-tuple-element.10), channel_id=1, source_target_pairs={{0,1},{1,2},{2,3},{3,4},{4,5},{5,6},{6,7},{7,8},{8,9},{9,10},{10,1... | collective-permute-start | bytes 884744 | tf_op jit(solution)/shard_map/ppermute | solution.py:403
  74.0 12.5 %collective-permute-start.1 = (bf16[8,144,128]{2,1,0:T(8,128)(2,1)}, bf16[8,144,128]{2,1,0:T(8,128)(2,1)S(1)}, u32[]{:S(2)}, u32[]{:S(2)}) collective-permute-start(bf16[8,144,128]{2,1,0:T(8,128)(2,1)} %get-tuple-element.11), channel_id=1, source_target_pairs={{0,15},{1,0},{2,1},{3,2},{4,3},{5,4},{6,5},{7,6},{8,7},{9,8},{10,9... | collective-permute-start | bytes 884744 | tf_op jit(solution)/shard_map/ppermute | solution.py:403
  86.5 12.0 %copy-start = (bf16[8,144,128]{2,1,0:T(8,128)(2,1)}, bf16[8,144,128]{2,1,0:T(8,128)(2,1)S(1)}, u32[]{:S(2)}) copy-start(bf16[8,144,128]{2,1,0:T(8,128)(2,1)S(1)} %collective-permute-done.refs_2_) | copy-start | bytes 884740
  86.5 12.0 %copy-start.1 = (bf16[8,144,128]{2,1,0:T(8,128)(2,1)}, bf16[8,144,128]{2,1,0:T(8,128)(2,1)S(1)}, u32[]{:S(2)}) copy-start(bf16[8,144,128]{2,1,0:T(8,128)(2,1)S(1)} %collective-permute-done.1.refs_3_) | copy-start | bytes 884740
  86.6 11.9 %collective-permute-start.2 = (bf16[10,144,128]{2,1,0:T(8,128)(2,1)S(1)}, bf16[10,144,128]{2,1,0:T(8,128)(2,1)S(1)}, u32[]{:S(2)}, u32[]{:S(2)}) collective-permute-start(bf16[10,144,128]{2,1,0:T(8,128)(2,1)S(1)} %pad_maximum_fusion), channel_id=1, source_target_pairs={{0,16},{16,32},{32,48},{48,64},{64,80},{80,96},{96,112},{1,17},{17... | collective-permute-start | bytes 1105928 | tf_op jit(solution)/shard_map/ppermute | solution.py:403
  89.6 9.0 %collective-permute-start.3 = (bf16[10,144,128]{2,1,0:T(8,128)(2,1)S(1)}, bf16[10,144,128]{2,1,0:T(8,128)(2,1)}, u32[]{:S(2)}, u32[]{:S(2)}) collective-permute-start(bf16[10,144,128]{2,1,0:T(8,128)(2,1)S(1)} %pad_maximum_fusion.1), channel_id=1, source_target_pairs={{16,0},{32,16},{48,32},{64,48},{80,64},{96,80},{112,96},{17,1},{33... | collective-permute-start | bytes 1105928 | tf_op jit(solution)/shard_map/ppermute | solution.py:403
  98.5 0.7 copy-start.2

commit v5 on v4

--- a/solution.py
+++ b/solution.py
@@ -422,11 +422,11 @@
     half = lat // 2
     inner = [
         [(r, c) for r in rows for c in range(1, lon - 1)]
-        for rows in (range(1, half), range(half, lat - 1))
+        for rows in (range(1, half + 1), range(half + 1, lat - 1))
     ]
     ready = [
-        inner_transforms(gh, loc_pattern, [sites], start, half + 1, devices, lon)
-        for sites, start in zip(inner, (0, half - 1))
+        inner_transforms(gh, loc_pattern, [sites], start, depth, devices, lon)
+        for sites, start, depth in zip(inner, (0, half), (half + 2, lat - half))
     ]
     rim = [
         [(r, c) for r in rows for c in range(lon) if (r, c) not in inner[0] + inner[1]]

time: 175 us -> 174 us (level)
  blocking collectives: 124 us -> 122 us
  transfers between devices with their start and end apart: 4 -> 4, of which waited for: 0 -> 1; matrix products, arithmetic and copies ran while one was open for 1% -> 1% of each run, Pallas kernels for 8% -> 8%
where the time goes in v5:
time: 174 us; the launch traced here: 173 us
  blocking collectives  122 us (70%)
  Pallas kernels  33.5 us (19%)
  starting transfers between devices  9.82 us (6%)
  local copies, waits for them, and re-layouts  6.46 us (4%)
    all_to_all x1, blocking collectives, shards(): lax.all_to_all(tiled.reshape(devices, lat * lon, cells), AXES, split_axis...  64.1 us
    all_to_all x1, blocking collectives, shards(): back = lax.all_to_all(result, AXES, split_axis=0, concat_axis=0, tiled=True)  58 us
    pallas_call x2, Pallas kernels, inner_transforms(): pl.pallas_call(kernel, in_specs=[pl.BlockSpec(memory_space=pltpu.VMEM), p...  14 us
    pallas_call x1, Pallas kernels, analyse(): pl.pallas_call(kernel, in_specs=[pl.BlockSpec(memory_space=pltpu.VMEM)] +...  12.5 us
    ppermute x4, starting transfers between devices, shift(): return lax.ppermute(value, axis, pairs)  9.82 us
    pallas_call x1, Pallas kernels, select(): pl.pallas_call(kernel, grid=(blocks // group,), in_specs=[pl.BlockSpec((m...  6.92 us
  transfers between devices with their start and end apart: 4, of which 1 were waited for; matrix products, arithmetic and copies ran while one was open for 1% of the time, Pallas kernels for 8%

profile of v5, /device:TPU:1, one launch (start us, length us, event | category | flops | bytes accessed | tf_op | source)
XLA Modules:
  0.0 173.0 jit_solution(17293060136759849794)
XLA Ops:
  0.0 2.8 %copy.7 = bf16[8,8,16,8,256]{4,3,1,2,0:T(8,128)(2,1)S(1)} copy(bf16[8,8,16,8,256]{4,3,2,1,0:T(8,128)(2,1)} %bitcast.11) | data formatting | bytes 8388608 | tf_op jit(solution)/shard_map/reshape | solution.py:414
  2.8 64.1 %all_to_all.10.x_ref = bf16[128,64,256]{2,1,0:T(8,128)(2,1)} all-to-all(bf16[128,64,256]{2,1,0:T(8,128)(2,1)S(1)} %bitcast.10), channel_id=1, replica_groups=mesh['mem'=8,'blk'=16] {'mem','blk'}, dimensions={0} | all-to-all | bytes 8388608 | tf_op jit(solution)/shard_map/all_to_all | solution.py:415
  66.8 6.9 %select.1 = (bf16[64,128,256]{2,1,0:T(8,128)(2,1)}, bf16[64,144,128]{2,1,0:T(8,128)(2,1)}, bf16[8,144,128]{2,1,0:T(8,128)(2,1)}, bf16[8,144,128]{2,1,0:T(8,128)(2,1)}) custom-call(bf16[128,64,256]{2,1,0:T(8,128)(2,1)} %all_to_all.10.x_ref, s32[8,8,128]{2,1,0:T(8,128)} %cell_ref.1, f32[8,8,128]{2,1,0:T(8,128)} %value_ref.1, f32[8,8,128]{2,1,0:T(8,128)} %rinv_ref.1, ...), custom_call_target="tpu_custom_call" | custom-call | flops 19008000000 | bytes 64000 | tf_op jit(solution)/shard_map/select/pallas_call | solution.py:84
  73.8 0.2 collective-permute-start
  74.0 4.6 %collective-permute-start.1 = (bf16[8,144,128]{2,1,0:T(8,128)(2,1)}, bf16[8,144,128]{2,1,0:T(8,128)(2,1)S(1)}, u32[]{:S(2)}, u32[]{:S(2)}) collective-permute-start(bf16[8,144,128]{2,1,0:T(8,128)(2,1)} %get-tuple-element.11), channel_id=1, source_target_pairs={{0,15},{1,0},{2,1},{3,2},{4,3},{5,4},{6,5},{7,6},{8,7},{9,8},{10,9... | collective-permute-start | bytes 884744 | tf_op jit(solution)/shard_map/ppermute | solution.py:403
  78.6 8.2 %inner_transforms.2.refs_7_ = bf16[24,128,128]{2,1,0:T(8,128)(2,1)} custom-call(s32[8,8,9]{2,1,0:T(8,128)} %refs_0_.1, bf16[8,8,144,128]{3,2,1,0:T(8,128)(2,1)} %bitcast.12), custom_call_target="tpu_custom_call" | custom-call | flops 10560000000 | bytes 24000 | tf_op jit(solution)/shard_map/inner_transforms/pallas_call | solution.py:238
  86.8 1.1 fusion
  87.9 0.0 collective-permute-done.refs_2_
  87.9 0.0 copy-start
  87.9 0.0 collective-permute-done.1.refs_3_
  87.9 0.0 copy-start.1
  87.9 0.1 pad_maximum_fusion
  88.0 2.9 %collective-permute-start.2 = (bf16[10,144,128]{2,1,0:T(8,128)(2,1)S(1)}, bf16[10,144,128]{2,1,0:T(8,128)(2,1)S(1)}, u32[]{:S(2)}, u32[]{:S(2)}) collective-permute-start(bf16[10,144,128]{2,1,0:T(8,128)(2,1)S(1)} %pad_maximum_fusion), channel_id=1, source_target_pairs={{0,16},{16,32},{32,48},{48,64},{64,80},{80,96},{96,112},{1,17},{17... | collective-permute-start | bytes 1105928 | tf_op jit(solution)/shard_map/ppermute | solution.py:403
  90.9 0.1 pad_maximum_fusion.1
  91.0 2.1 %collective-permute-start.3 = (bf16[10,144,128]{2,1,0:T(8,128)(2,1)S(1)}, bf16[10,144,128]{2,1,0:T(8,128)(2,1)}, u32[]{:S(2)}, u32[]{:S(2)}) collective-permute-start(bf16[10,144,128]{2,1,0:T(8,128)(2,1)S(1)} %pad_maximum_fusion.1), channel_id=1, source_target_pairs={{16,0},{32,16},{48,32},{64,48},{80,64},{96,80},{112,96},{17,1},{33... | collective-permute-start | bytes 1105928 | tf_op jit(solution)/shard_map/ppermute | solution.py:403
  93.1 5.8 %inner_transforms.3.refs_8_ = bf16[12,128,128]{2,1,0:T(8,128)(2,1)} custom-call(s32[8,8,9]{2,1,0:T(8,128)} %refs_0_.1, bf16[8,8,144,128]{3,2,1,0:T(8,128)(2,1)} %bitcast.13), custom_call_target="tpu_custom_call" | custom-call | flops 5280000000 | bytes 12000 | tf_op jit(solution)/shard_map/inner_transforms/pallas_call | solution.py:238
  98.9 0.0 copy-done
  98.9 0.0 copy-done.1
  98.9 0.0 collective-permute-done.2.refs_5_
  99.0 0.0 copy-start.2
  99.0 1.0 collective-permute-done.3.refs_6_
  99.9 0.0 copy-done.2
  99.9 12.5 %analyse.1 = bf16[128,64,256]{2,1,0:T(8,128)(2,1)} custom-call(s32[8,8,9]{2,1,0:T(8,128)} %refs_0_.1, bf16[8,8,144,128]{3,2,1,0:T(8,128)(2,1)} %bitcast.14, bf16[8,144,128]{2,1,0:T(8,128)(2,1)} %copy-done, bf16[8,144,128]{2,1,0:T(8,128)(2,1)} %copy-done.1, bf16[64,128,256]{2,1,0:T(8,128)(2,1)} %get-tuple-element.12.refs_4_, bf16[10,144,128]{2,1,0:T(8,128)(2,1)} %copy-done.2, ...), custom_call_target="tpu_custom_call" | custom-call | flops 24640000000 | bytes 64000 | tf_op jit(solution)/shard_map/analyse/pallas_call | solution.py:375
  112.5 58.0 %all_to_all.11 = bf16[128,64,256]{2,1,0:T(8,128)(2,1)S(1)} all-to-all(bf16[128,64,256]{2,1,0:T(8,128)(2,1)} %analyse.1), channel_id=1, replica_groups=mesh['mem'=8,'blk'=16] {'mem','blk'}, dimensions={0} | all-to-all | bytes 8388608 | tf_op jit(solution)/shard_map/all_to_all | solution.py:444
  170.5 2.6 %copy.8 = bf16[8,8,16,8,256]{4,3,2,1,0:T(8,128)(2,1)} copy(bf16[8,8,16,8,256]{4,3,1,2,0:T(8,128)(2,1)S(1)} %bitcast.9) | data formatting | bytes 8388608 | tf_op jit(solution)/shard_map/transpose | solution.py:445
  (2 shorter events, 0.0 us)
Async XLA Ops:
  73.8 14.1 %collective-permute-start = (bf16[8,144,128]{2,1,0:T(8,128)(2,1)}, bf16[8,144,128]{2,1,0:T(8,128)(2,1)S(1)}, u32[]{:S(2)}, u32[]{:S(2)}) collective-permute-start(bf16[8,144,128]{2,1,0:T(8,128)(2,1)} %get-tuple-element.10), channel_id=1, source_target_pairs={{0,1},{1,2},{2,3},{3,4},{4,5},{5,6},{6,7},{7,8},{8,9},{9,10},{10,1... | collective-permute-start | bytes 884744 | tf_op jit(solution)/shard_map/ppermute | solution.py:403
  74.0 14.0 %collective-permute-start.1 = (bf16[8,144,128]{2,1,0:T(8,128)(2,1)}, bf16[8,144,128]{2,1,0:T(8,128)(2,1)S(1)}, u32[]{:S(2)}, u32[]{:S(2)}) collective-permute-start(bf16[8,144,128]{2,1,0:T(8,128)(2,1)} %get-tuple-element.11), channel_id=1, source_target_pairs={{0,15},{1,0},{2,1},{3,2},{4,3},{5,4},{6,5},{7,6},{8,7},{9,8},{10,9... | collective-permute-start | bytes 884744 | tf_op jit(solution)/shard_map/ppermute | solution.py:403
  87.9 11.0 %copy-start = (bf16[8,144,128]{2,1,0:T(8,128)(2,1)}, bf16[8,144,128]{2,1,0:T(8,128)(2,1)S(1)}, u32[]{:S(2)}) copy-start(bf16[8,144,128]{2,1,0:T(8,128)(2,1)S(1)} %collective-permute-done.refs_2_) | copy-start | bytes 884740
  87.9 11.0 %copy-start.1 = (bf16[8,144,128]{2,1,0:T(8,128)(2,1)}, bf16[8,144,128]{2,1,0:T(8,128)(2,1)S(1)}, u32[]{:S(2)}) copy-start(bf16[8,144,128]{2,1,0:T(8,128)(2,1)S(1)} %collective-permute-done.1.refs_3_) | copy-start | bytes 884740
  88.0 10.9 %collective-permute-start.2 = (bf16[10,144,128]{2,1,0:T(8,128)(2,1)S(1)}, bf16[10,144,128]{2,1,0:T(8,128)(2,1)S(1)}, u32[]{:S(2)}, u32[]{:S(2)}) collective-permute-start(bf16[10,144,128]{2,1,0:T(8,128)(2,1)S(1)} %pad_maximum_fusion), channel_id=1, source_target_pairs={{0,16},{16,32},{32,48},{48,64},{64,80},{80,96},{96,112},{1,17},{17... | collective-permute-start | bytes 1105928 | tf_op jit(solution)/shard_map/ppermute | solution.py:403
  91.0 8.9 %collective-permute-start.3 = (bf16[10,144,128]{2,1,0:T(8,128)(2,1)S(1)}, bf16[10,144,128]{2,1,0:T(8,128)(2,1)}, u32[]{:S(2)}, u32[]{:S(2)}) collective-permute-start(bf16[10,144,128]{2,1,0:T(8,128)(2,1)S(1)} %pad_maximum_fusion.1), channel_id=1, source_target_pairs={{16,0},{32,16},{48,32},{64,48},{80,64},{96,80},{112,96},{17,1},{33... | collective-permute-start | bytes 1105928 | tf_op jit(solution)/shard_map/ppermute | solution.py:403
  99.0 1.0 copy-start.2
